TPU v7x, 128 devices: a whole 4x4x4 slice. The times are simulated.
128 devices in a mesh: replica: 4 (over y_lo, core), expert: 32 (over y_hi, z, x).
Axes of the slice: x: 4, y: 4 (y_hi: 2, y_lo: 2; y = y_hi * 2 + y_lo), z: 4, core: 2. Of those that a mesh axis runs over, the one named last changes fastest.
Arguments:
- hidden_in: bfloat16 [2048, 4096], P(('replica', 'expert')), may hold values from -6 to 6
- query: bfloat16 [2048, 8192], P(('replica', 'expert')), may hold values from -50 to 50
- key_new: bfloat16 [2048, 512], P(('replica', 'expert')), may hold values from -6 to 6
- value_new: bfloat16 [2048, 512], P(('replica', 'expert')), may hold values from -6 to 6
- key_cache: bfloat16 [2048, 4, 512, 128], P(('replica', 'expert')), may hold values from -6 to 6
- value_cache: bfloat16 [2048, 4, 512, 128], P(('replica', 'expert')), may hold values from -6 to 6
- cache_len: int32 [2048], P(('replica', 'expert')), may hold values from 2 to 512, as said below
- attn_out_w: bfloat16 [8192, 4096], P('expert', 'replica'), may hold values from -0.0625 to 0.0625
- norm_gain: float32 [4096], replicated, may hold values from 0.5 to 2
- routes: int32 [2048, 8], P(('replica', 'expert')), may hold values from 0 to 31, all different within a row; in each aligned block of 16 rows (0 to 15, 16 to 31, ...) at most 8 rows name the same one
- gate_weights: float32 [2048, 8], P(('replica', 'expert')), may hold values from 0.05 to 0.4
- w_gate: bfloat16 [32, 4096, 1536], P('expert', 'replica'), may hold values from -0.09375 to 0.09375
- w_up: bfloat16 [32, 4096, 1536], P('expert', 'replica'), may hold values from -0.09375 to 0.09375
- w_down: bfloat16 [32, 1536, 4096], P('expert', None, 'replica'), may hold values from -0.15625 to 0.15625
Outputs:
- layer_out: bfloat16 [2048, 4096], P(('replica', 'expert'))
Inputs may be any that keep to these rules, and one draw needn't show every extreme that they name: `routes`: each row names 8 different experts; among the rows of one device no expert is named by more than 8 rows. `cache_len`: every row has at least two cached positions; some row has all 512.
All inputs are finite; a program needn't handle non-finite values.
Results may differ from a plain program's by a relative error of at most 0.015.
Values may be sent and summed in bfloat16 or wider, within the bound.
A program may use at most 192 MiB of HBM per device.

v0:
```python
import jax
import jax.numpy as jnp
from jax import lax
from jax.sharding import PartitionSpec as P

HD = 128
TOP = 8
EXPERTS = 32
CAP = 8


def attend_local(query, key_new, value_new, key_cache, value_cache, cache_len):
    rows = query.shape[0]
    kv_heads = key_cache.shape[1]
    context = key_cache.shape[2]
    head_size = key_cache.shape[3]
    grouped = query.shape[1] // (kv_heads * head_size)
    scale = HD ** (-0.5)
    queries = query.reshape(rows, kv_heads, grouped, head_size)
    cached = (
        jnp.einsum("rgqd,rgpd->rgqp", queries, key_cache, preferred_element_type=jnp.float32)
        * scale
    )
    own = (
        jnp.einsum(
            "rgqd,rgd->rgq",
            queries,
            key_new.reshape(rows, kv_heads, head_size),
            preferred_element_type=jnp.float32,
        )
        * scale
    )
    live = jnp.arange(context)[None, :] < cache_len[:, None]
    cached = jnp.where(live[:, None, None, :], cached, -jnp.inf)
    highest = jnp.maximum(jnp.max(cached, axis=-1), own)
    cached_exp = jnp.exp(cached - highest[..., None])
    own_exp = jnp.exp(own - highest)
    total = jnp.sum(cached_exp, axis=-1) + own_exp
    cached_prob = (cached_exp / total[..., None]).astype(jnp.bfloat16)
    own_prob = (own_exp / total).astype(jnp.bfloat16)
    mixed = jnp.einsum(
        "rgqp,rgpd->rgqd", cached_prob, value_cache, preferred_element_type=jnp.float32
    )
    mixed = mixed + own_prob.astype(jnp.float32)[..., None] * value_new.reshape(
        rows, kv_heads, 1, head_size
    ).astype(jnp.float32)
    return mixed.reshape(rows, grouped * kv_heads * head_size).astype(jnp.bfloat16)


def send_back(values):
    return lax.all_to_all(values, "expert", split_axis=1, concat_axis=1, tiled=True)


def body(
    hidden_in,
    query,
    key_new,
    value_new,
    key_cache,
    value_cache,
    cache_len,
    attn_out_w,
    norm_gain,
    routes,
    gate_weights,
    w_gate,
    w_up,
    w_down,
):
    rows_dev = hidden_in.shape[0]
    width = hidden_in.shape[1]
    n_expert = lax.axis_size("expert")
    local_experts = w_gate.shape[0]
    all_slots = EXPERTS * CAP
    attn = attend_local(query, key_new, value_new, key_cache, value_cache, cache_len)
    head_rows = lax.all_to_all(attn, "expert", split_axis=1, concat_axis=0, tiled=True)
    out_proj = lax.all_gather(attn_out_w, "replica", axis=1, tiled=True)
    mid = hidden_in.astype(jnp.float32) + lax.psum_scatter(
        jnp.dot(head_rows, out_proj, preferred_element_type=jnp.float32).astype(jnp.bfloat16),
        "expert",
        scatter_dimension=0,
        tiled=True,
    ).astype(jnp.float32)
    normed = (
        mid * lax.rsqrt(jnp.mean(mid * mid, axis=-1, keepdims=True) + 1e-06) * norm_gain
    ).astype(jnp.bfloat16)
    flat = routes.reshape(-1)
    onehot = (flat[:, None] == jnp.arange(EXPERTS)[None, :]).astype(jnp.int32)
    rank = jnp.sum((jnp.cumsum(onehot, axis=0) - 1) * onehot, axis=1)
    target = flat % local_experts * (n_expert * CAP) + flat // local_experts * CAP + rank
    chosen = (target[:, None] == jnp.arange(all_slots)[None, :]).reshape(rows_dev, TOP, all_slots)
    placing = jnp.any(chosen, axis=1).astype(jnp.bfloat16)
    outgoing = lax.dot_general(
        placing, normed, (((0,), (0,)), ((), ())), preferred_element_type=jnp.float32
    )
    outgoing = outgoing.astype(jnp.bfloat16).reshape(local_experts, n_expert, CAP, width)
    gate_full, up_full, down_full = (
        lax.all_gather(w_gate, "replica", axis=1, tiled=True),
        lax.all_gather(w_up, "replica", axis=1, tiled=True),
        lax.all_gather(w_down, "replica", axis=2, tiled=True),
    )
    block = lax.all_to_all(outgoing, "expert", split_axis=1, concat_axis=1, tiled=True)
    gate = jnp.einsum("lncd,ldh->lnch", block, gate_full, preferred_element_type=jnp.float32)
    up_val = jnp.einsum("lncd,ldh->lnch", block, up_full, preferred_element_type=jnp.float32)
    units = (jax.nn.silu(gate) * up_val).astype(jnp.bfloat16)
    result = jnp.einsum(
        "lnch,lhd->lncd", units, down_full, preferred_element_type=jnp.float32
    ).astype(jnp.bfloat16)
    returned = send_back(result)
    weighting = jnp.sum(chosen.astype(jnp.float32) * gate_weights[:, :, None], axis=1)
    mixture = jnp.dot(
        weighting,
        returned.reshape(all_slots, width).astype(jnp.float32),
        precision=lax.Precision.HIGHEST,
    )
    return (mid + mixture).astype(jnp.bfloat16)


def solution(mesh):
    placed = (
        P(("replica", "expert"), None),
        P(("replica", "expert"), None),
        P(("replica", "expert"), None),
        P(("replica", "expert"), None),
        P(("replica", "expert"), None, None, None),
        P(("replica", "expert"), None, None, None),
        P(("replica", "expert")),
        P("expert", "replica"),
        P(),
        P(("replica", "expert"), None),
        P(("replica", "expert"), None),
        P("expert", "replica", None),
        P("expert", "replica", None),
        P("expert", None, "replica"),
    )
    return jax.shard_map(
        body, mesh=mesh, in_specs=placed, out_specs=P(("replica", "expert"), None), check_vma=False
    )
```

profile of v0, /device:TPU:0, one launch (start us, length us, event | category | flops | bytes accessed | tf_op | source)
XLA Modules:
  0.0 667.3 jit_solution(8338262118293983854)
XLA Ops:
  6.5 0.0 all-gather.5.cloned.1.call-start
  6.5 0.7 all-gather.5.cloned.1.call-update
  7.3 0.0 reduce-scatter.2.cloned.1.call-start
  7.3 1.0 copy.36
  8.3 0.7 reshape.119
  9.0 0.7 reshape.112
  9.8 0.7 iota_compare_fusion.2
  10.5 0.3 fusion.49
  10.8 5.9 fusion.26
  16.7 0.8 fusion.27
  17.5 1.5 fusion.33
  19.1 0.1 convert_element_type.68
  19.2 0.2 copy.28
  19.3 21.2 %all_to_all.26 = bf16[16,32,256]{2,0,1:T(8,128)(2,1)S(1)} all-to-all(bf16[16,32,256]{2,0,1:T(8,128)(2,1)S(1)} %copy.28), channel_id=1, replica_groups=mesh['replica'=4,'expert'=32] {'expert'}, dimensions={1} | all-to-all | bytes 524288 | tf_op jit(solution)/shard_map/all_to_all | solution.py:76
  40.5 2.8 all-gather.5.cloned.1.call-done
  43.3 4.8 convolution_convert_fusion
  48.1 0.0 reduce-scatter.2.cloned.1.call-update
  48.1 0.0 all-gather.7.cloned.1.call-start
  48.1 0.7 all-gather.7.cloned.1.call-update
  48.8 0.0 all-gather.11.cloned.1.call-start
  48.9 0.5 all-gather.11.cloned.1.call-update
  49.4 0.0 copy-start.3
  49.4 0.0 copy-start
  49.4 0.0 copy-start.2
  49.4 0.0 all-gather.9.cloned.1.call-start
  49.5 0.5 all-gather.9.cloned.1.call-update
  50.0 0.1 copy-done.3
  50.1 0.1 copy.29
  50.2 0.1 eq.31
  50.2 0.1 fusion.43
  50.3 0.2 reduce_window_sum.11
  50.5 0.2 select_reduce_fusion.1
  50.7 0.1 reduce_sum.40
  50.8 0.1 fusion.42
  50.9 193.7 %reduce-scatter.2.cloned.1.call-done = bf16[16,4096]{1,0:T(8,128)(2,1)} async-done(((bf16[512,4096]{1,0:T(8,128)(2,1)}), bf16[16,4096]{1,0:T(8,128)(2,1)}) %reduce-scatter.2.cloned.1.call-update) | async-done | bytes 131088 | tf_op jit(solution)/shard_map/reduce_scatter | solution.py:78
  244.6 1.1 multiply_reduce_fusion
  245.7 1.7 fusion.12
  247.4 22.7 %all_to_all.27 = bf16[1,32,8,4096]{3,2,0,1:T(8,128)(2,1)S(1)} all-to-all(bf16[1,32,8,4096]{3,2,0,1:T(8,128)(2,1)S(1)} %fusion.12), channel_id=1, replica_groups=mesh['replica'=4,'expert'=32] {'expert'}, dimensions={1} | all-to-all | bytes 4194304 | tf_op jit(solution)/shard_map/all_to_all | solution.py:102
  270.1 94.9 %all-gather.7.cloned.1.call-done = bf16[1,4096,1536]{2,1,0:T(8,128)(2,1)} async-done(((bf16[1,1024,1536]{2,1,0:T(8,128)(2,1)}), bf16[1,4096,1536]{2,1,0:T(8,128)(2,1)}) %all-gather.7.cloned.1.call-update) | async-done | bytes 12582928 | tf_op jit(solution)/shard_map/all_gather | solution.py:98
  365.0 7.6 %fusion.4 = f32[32,8,1536]{2,1,0:T(8,128)} fusion(bf16[1,4096,1536]{2,1,0:T(8,128)(2,1)} %all-gather.7.cloned.1.call-done, bf16[1,32,8,4096]{3,2,0,1:T(8,128)(2,1)S(1)} %all_to_all.27), kind=kOutput, calls=%fused_computation.4 | convolution fusion | flops 3221225472 | bytes 16252928 | tf_op jit(solution)/shard_map/lncd,ldh->lnch/dot_general | solution.py:103
  372.6 110.4 %all-gather.11.cloned.1.call-done = bf16[1,1536,4096]{2,1,0:T(8,128)(2,1)} async-done(((bf16[1,1536,1024]{2,1,0:T(8,128)(2,1)}), bf16[1,1536,4096]{2,1,0:T(8,128)(2,1)}) %all-gather.11.cloned.1.call-update) | async-done | bytes 12582928 | tf_op jit(solution)/shard_map/all_gather | solution.py:100
  483.0 118.7 %all-gather.9.cloned.1.call-done = bf16[1,4096,1536]{2,1,0:T(8,128)(2,1)} async-done(((bf16[1,1024,1536]{2,1,0:T(8,128)(2,1)}), bf16[1,4096,1536]{2,1,0:T(8,128)(2,1)}) %all-gather.9.cloned.1.call-update) | async-done | bytes 12582928 | tf_op jit(solution)/shard_map/all_gather | solution.py:99
  601.7 16.7 %fusion.9 = bf16[1,32,8,4096]{3,2,0,1:T(8,128)(2,1)} fusion(bf16[1,1536,4096]{2,1,0:T(8,128)(2,1)} %all-gather.11.cloned.1.call-done, bf16[1,4096,1536]{2,1,0:T(8,128)(2,1)} %all-gather.9.cloned.1.call-done, bf16[1,32,8,4096]{3,2,0,1:T(8,128)(2,1)S(1)} %all_to_all.27, f32[32,8,1536]{2,1,0:T(8,128)} %fusion.4), kind=kOutput, calls=%fused_computation.9 | convolution fusion | flops 6445858816 | bytes 30932992 | tf_op jit(solution)/shard_map/lnch,lhd->lncd/dot_general | solution.py:106
  618.4 10.0 %all-to-all-start.2 = ((bf16[1,32,8,4096]{3,2,0,1:T(8,128)(2,1)}), bf16[1,32,8,4096]{3,2,0,1:T(8,128)(2,1)S(1)}, u32[]{:S(2)}, u32[]{:S(2)}) async-start(bf16[1,32,8,4096]{3,2,0,1:T(8,128)(2,1)} %fusion.9), calls=%async_computation.3 | async-start | bytes 4194304 | tf_op jit(solution)/shard_map/all_to_all | solution.py:51
  628.4 0.1 copy.31
  628.4 0.1 select_reduce_fusion
  628.6 30.6 %all-to-all-done.2 = bf16[1,32,8,4096]{3,2,0,1:T(8,128)(2,1)S(1)} async-done(((bf16[1,32,8,4096]{3,2,0,1:T(8,128)(2,1)}), bf16[1,32,8,4096]{3,2,0,1:T(8,128)(2,1)S(1)}, u32[]{:S(2)}, u32[]{:S(2)}) %all-to-all-start.2) | async-done | bytes 2097184 | tf_op jit(solution)/shard_map/all_to_all | solution.py:51
  659.2 1.6 fusion.13
  (12 shorter events, 0.1 us)
Async XLA Ops:
  6.5 36.7 %all-gather.5.cloned.1.call-start = ((), (), s32[]{:S(2)}) async-start(), calls=%async_computation.4 | async-start | bytes 2621440 | tf_op jit(solution)/shard_map/all_gather | solution.py:77
  7.3 237.4 %reduce-scatter.2.cloned.1.call-start = ((), (), s32[]{:S(2)}) async-start(), calls=%async_computation.5 | async-start | bytes 4325376 | tf_op jit(solution)/shard_map/reduce_scatter | solution.py:78
  10.8 6.8 %copy-start.5 = (bf16[16,4,512,128]{3,2,1,0:T(8,128)(2,1)S(1)}, bf16[16,4,512,128]{3,2,1,0:T(8,128)(2,1)}, u32[]{:S(2)}) copy-start(bf16[16,4,512,128]{3,2,1,0:T(8,128)(2,1)} %param.19) | copy-start | bytes 25165828
  48.1 316.9 %all-gather.7.cloned.1.call-start = ((), (), s32[]{:S(2)}) async-start(), calls=%async_computation.6 | async-start | bytes 15728640 | tf_op jit(solution)/shard_map/all_gather | solution.py:98
  48.8 434.2 %all-gather.11.cloned.1.call-start = ((), (), s32[]{:S(2)}) async-start(), calls=%async_computation.8 | async-start | bytes 15728640 | tf_op jit(solution)/shard_map/all_gather | solution.py:100
  49.4 0.7 copy-start.3
  49.4 195.2 %copy-start = (bf16[16,4096]{1,0:T(8,128)(2,1)S(1)}, bf16[16,4096]{1,0:T(8,128)(2,1)}, u32[]{:S(2)}) copy-start(bf16[16,4096]{1,0:T(8,128)(2,1)} %param.14) | copy-start | bytes 393220
  49.4 196.3 %copy-start.2 = (f32[4096]{0:T(1024)S(1)}, f32[4096]{0:T(1024)}, u32[]{:S(2)}) copy-start(f32[4096]{0:T(1024)} %param.22) | copy-start | bytes 49156
  49.4 552.3 %all-gather.9.cloned.1.call-start = ((), (), s32[]{:S(2)}) async-start(), calls=%async_computation.7 | async-start | bytes 15728640 | tf_op jit(solution)/shard_map/all_gather | solution.py:99
  618.4 10.0 %copy-start.4 = (f32[16,8]{0,1:T(8,128)S(1)}, f32[16,8]{0,1:T(8,128)}, u32[]{:S(2)}) copy-start(f32[16,8]{0,1:T(8,128)} %param.24) | copy-start | bytes 1540
  618.4 40.8 %copy-start.1 = (bf16[16,4096]{1,0:T(8,128)(2,1)S(1)}, bf16[16,4096]{1,0:T(8,128)(2,1)}, u32[]{:S(2)}) copy-start(bf16[16,4096]{1,0:T(8,128)(2,1)} %reduce-scatter.2.cloned.1.call-done) | copy-start | bytes 393220
  618.4 40.8 %all-to-all-start.2 = ((bf16[1,32,8,4096]{3,2,0,1:T(8,128)(2,1)}), bf16[1,32,8,4096]{3,2,0,1:T(8,128)(2,1)S(1)}, u32[]{:S(2)}, u32[]{:S(2)}) async-start(bf16[1,32,8,4096]{3,2,0,1:T(8,128)(2,1)} %fusion.9), calls=%async_computation.3 | async-start | bytes 4194304 | tf_op jit(solution)/shard_map/all_to_all | solution.py:51
Sparse Core Ops, SparseCore 0:
  9.0 34.1 all-gather.4
  48.2 196.3 reduce-scatter.1
  246.3 118.6 all-gather.6
  366.5 116.4 all-gather.10
  484.5 117.1 all-gather.8
where the time goes:
time: 670 us; the launch traced here: 667 us
  waiting for transfers between devices  554 us (83%)
  blocking collectives  43.9 us (7%)
  matrix products  40 us (6%)
  between operations  13.3 us (2%)
  starting transfers between devices  10.1 us (2%)
    reduce_scatter x1, waiting for transfers between devices, body(): lax.psum_scatter(jnp.dot(head_rows, out_proj, preferred_element_type=jnp....  194 us
    all_gather x1, waiting for transfers between devices, body(): lax.all_gather(w_up, 'replica', axis=1, tiled=True)  119 us
    all_gather x1, waiting for transfers between devices, body(): lax.all_gather(w_down, 'replica', axis=2, tiled=True)  110 us
    all_gather x1, waiting for transfers between devices, body(): lax.all_gather(w_gate, 'replica', axis=1, tiled=True)  94.9 us
    all_to_all x1, waiting for transfers between devices, send_back(): lax.all_to_all(values, 'expert', split_axis=1, concat_axis=1, tiled=True)  30.6 us
    all_to_all x1, blocking collectives, body(): lax.all_to_all(outgoing, 'expert', split_axis=1, concat_axis=1, tiled=True)  22.7 us
    all_to_all x1, blocking collectives, body(): lax.all_to_all(attn, 'expert', split_axis=1, concat_axis=0, tiled=True)  21.2 us
    dot_general x1, matrix products, body(): jnp.einsum('lnch,lhd->lncd', units, down_full, preferred_element_type=jnp...  16.7 us
  transfers between devices with their start and end apart: 6, of which 6 were waited for; matrix products, arithmetic and copies ran while one was open for 3% of the time, Pallas kernels for 0%

commit v1 on v0

v1 whole, which is shorter than its diff:
```python
import jax
import jax.numpy as jnp
from jax import lax
from jax.sharding import PartitionSpec as P

HD = 128
TOP = 8
EXPERTS = 32
CAP = 8
LINE = 4
GROUPS = 8
SWAP_Y = [(0, 2), (1, 3), (2, 0), (3, 1)]
SWAP_CORE = [(0, 1), (1, 0), (2, 3), (3, 2)]
SAME_X = [[x + LINE * a for a in range(GROUPS)] for x in range(LINE)]


def attend_local(query, key_new, value_new, key_cache, value_cache, cache_len):
    rows = query.shape[0]
    kv_heads = key_cache.shape[1]
    context = key_cache.shape[2]
    head_size = key_cache.shape[3]
    grouped = query.shape[1] // (kv_heads * head_size)
    scale = HD ** (-0.5)
    queries = query.reshape(rows, kv_heads, grouped, head_size)
    cached = (
        jnp.einsum("rgqd,rgpd->rgqp", queries, key_cache, preferred_element_type=jnp.float32)
        * scale
    )
    own = (
        jnp.einsum(
            "rgqd,rgd->rgq",
            queries,
            key_new.reshape(rows, kv_heads, head_size),
            preferred_element_type=jnp.float32,
        )
        * scale
    )
    live = jnp.arange(context)[None, :] < cache_len[:, None]
    cached = jnp.where(live[:, None, None, :], cached, -jnp.inf)
    highest = jnp.maximum(jnp.max(cached, axis=-1), own)
    cached_exp = jnp.exp(cached - highest[..., None])
    own_exp = jnp.exp(own - highest)
    total = jnp.sum(cached_exp, axis=-1) + own_exp
    cached_prob = (cached_exp / total[..., None]).astype(jnp.bfloat16)
    own_prob = (own_exp / total).astype(jnp.bfloat16)
    mixed = jnp.einsum(
        "rgqp,rgpd->rgqd", cached_prob, value_cache, preferred_element_type=jnp.float32
    )
    mixed = mixed + own_prob.astype(jnp.float32)[..., None] * value_new.reshape(
        rows, kv_heads, 1, head_size
    ).astype(jnp.float32)
    return mixed.reshape(rows, grouped * kv_heads * head_size).astype(jnp.bfloat16)


def swap_y(value):
    return lax.ppermute(value, "replica", SWAP_Y)


def swap_core(value):
    return lax.ppermute(value, "replica", SWAP_CORE)


def same_x(value):
    return lax.all_to_all(
        value, "expert", split_axis=0, concat_axis=0, axis_index_groups=SAME_X, tiled=True
    )


def from_x(value, step):
    pairs = [
        (e, e // LINE * LINE + (e + LINE - step) % LINE) for e in range(EXPERTS)
    ]
    return lax.ppermute(value, "expert", pairs)


def relative(quarters, replica):
    core, chip = replica % 2, replica // 2
    a, b, c, d = quarters
    a, b, c, d = (
        jnp.where(core == 0, a, b),
        jnp.where(core == 0, b, a),
        jnp.where(core == 0, c, d),
        jnp.where(core == 0, d, c),
    )
    return (
        jnp.where(chip == 0, a, c),
        jnp.where(chip == 0, b, d),
        jnp.where(chip == 0, c, a),
        jnp.where(chip == 0, d, b),
    )


def body(
    hidden_in,
    query,
    key_new,
    value_new,
    key_cache,
    value_cache,
    cache_len,
    attn_out_w,
    norm_gain,
    routes,
    gate_weights,
    w_gate,
    w_up,
    w_down,
):
    f32, bf16 = jnp.float32, jnp.bfloat16
    rows = hidden_in.shape[0]
    width = hidden_in.shape[1]
    quarter = width // 4
    replica = lax.axis_index("replica")
    x = lax.axis_index("expert") % LINE

    proj = jnp.concatenate([attn_out_w] + [from_x(attn_out_w, s) for s in range(1, LINE)], axis=0)
    proj = jnp.concatenate([proj, swap_core(proj)], axis=1)
    gate_mats = (w_gate[0], swap_core(w_gate)[0])
    up_mats = (w_up[0], swap_core(w_up)[0])
    down_mats = (w_down[0], swap_core(w_down)[0])

    hid = relative([hidden_in[:, q * quarter : (q + 1) * quarter] for q in range(4)], replica)
    hid_here = jnp.concatenate(hid[:2], axis=1)
    hid_there = swap_y(jnp.concatenate(hid[2:], axis=1))
    hid = jnp.concatenate([hid_here, hid_there], axis=0).astype(f32)
    gain = relative([norm_gain[q * quarter : (q + 1) * quarter] for q in range(4)], replica)
    gain = jnp.concatenate(gain[:2])

    route2 = jnp.stack([routes, swap_y(routes)])
    weight2 = jnp.stack([gate_weights, swap_y(gate_weights)])
    flat = route2.reshape(2, rows * TOP)
    onehot = (flat[:, :, None] == jnp.arange(EXPERTS)[None, None, :]).astype(jnp.int32)
    rank = jnp.sum((jnp.cumsum(onehot, axis=1) - 1) * onehot, axis=2)
    target = (flat * CAP + rank).reshape(2, rows, TOP)
    chosen = target[..., None] == jnp.arange(EXPERTS * CAP)
    placing = jnp.any(chosen, axis=2).astype(bf16)
    weighting = jnp.sum(jnp.where(chosen, weight2[..., None], 0.0), axis=2)

    attn = attend_local(query, key_new, value_new, key_cache, value_cache, cache_len)
    heads = attn.reshape(rows, GROUPS, LINE, -1)
    heads = lax.dynamic_slice_in_dim(jnp.concatenate([heads, heads], axis=2), x, LINE, axis=2)
    heads = heads.reshape(rows, GROUPS, -1).transpose(1, 0, 2)
    heads = same_x(heads)
    heads = jnp.stack([heads, swap_y(heads)], axis=1)
    part = jnp.dot(heads.reshape(GROUPS * 2 * rows, -1), proj, preferred_element_type=f32)
    part = same_x(part.astype(bf16).reshape(GROUPS, 2 * rows, 2 * quarter))
    mid = hid + jnp.sum(part.astype(f32), axis=0)

    squares = jnp.sum(mid * mid, axis=-1)
    there = swap_y(squares)
    squares = squares + jnp.concatenate([there[rows:], there[:rows]])
    normed = (mid * lax.rsqrt(squares / width + 1e-06)[:, None] * gain).astype(bf16)

    outgoing = jnp.einsum(
        "hrs,hrd->hsd", placing, normed.reshape(2, rows, 2 * quarter), preferred_element_type=f32
    ).astype(bf16)
    outgoing = outgoing.reshape(2, EXPERTS, CAP, 2 * quarter).transpose(1, 0, 2, 3)
    block = lax.all_to_all(outgoing, "expert", split_axis=0, concat_axis=0, tiled=True)
    block = block.transpose(1, 0, 2, 3).reshape(2 * EXPERTS * CAP, 2 * quarter)
    ours, theirs = block[:, :quarter], block[:, quarter:]

    def partial(mats):
        return jnp.dot(ours, mats[0], preferred_element_type=f32) + jnp.dot(
            theirs, mats[1], preferred_element_type=f32
        )

    half = EXPERTS * CAP
    gate, up_val = partial(gate_mats), partial(up_mats)
    gate = gate[:half] + swap_y(gate[half:].astype(bf16)).astype(f32)
    up_val = up_val[:half] + swap_y(up_val[half:].astype(bf16)).astype(f32)
    units = (jax.nn.silu(gate) * up_val).astype(bf16)
    units = jnp.concatenate([units, swap_y(units)], axis=0)
    result = jnp.concatenate(
        [jnp.dot(units, mat, preferred_element_type=f32).astype(bf16) for mat in down_mats], axis=1
    )
    result = result.reshape(2, EXPERTS, CAP, 2 * quarter).transpose(1, 0, 2, 3)
    returned = lax.all_to_all(result, "expert", split_axis=0, concat_axis=0, tiled=True)
    returned = returned.transpose(1, 0, 2, 3).reshape(2, EXPERTS * CAP, 2 * quarter)
    mixture = jnp.einsum(
        "hrs,hsd->hrd", weighting, returned.astype(f32), precision=lax.Precision.HIGHEST
    )
    out = (mid + mixture.reshape(2 * rows, 2 * quarter)).astype(bf16)
    there = swap_y(out[rows:])
    here = out[:rows]
    return jnp.concatenate(
        relative(
            (here[:, :quarter], here[:, quarter:], there[:, :quarter], there[:, quarter:]), replica
        ),
        axis=1,
    )


def solution(mesh):
    placed = (
        P(("replica", "expert"), None),
        P(("replica", "expert"), None),
        P(("replica", "expert"), None),
        P(("replica", "expert"), None),
        P(("replica", "expert"), None, None, None),
        P(("replica", "expert"), None, None, None),
        P(("replica", "expert")),
        P("expert", "replica"),
        P(),
        P(("replica", "expert"), None),
        P(("replica", "expert"), None),
        P("expert", "replica", None),
        P("expert", "replica", None),
        P("expert", None, "replica"),
    )
    return jax.shard_map(
        body, mesh=mesh, in_specs=placed, out_specs=P(("replica", "expert"), None), check_vma=False
    )
```

time: 670 us -> 235 us (0.35)
  waiting for transfers between devices: 554 us -> 143 us
  blocking collectives: 43.9 us -> 0 us
  starting transfers between devices: 10.1 us -> 39.3 us
  between operations: 13.3 us -> 0.42 us
  local copies, waits for them, and re-layouts: 3.11 us -> 14.4 us
  matrix products: 40 us -> 33.1 us
    all_gather x4 -> x0, waiting for transfers between devices: 327 us -> none  [the longest x1 119 us: body(): lax.all_gather(w_up, 'replica', axis=1, tiled=True)]
    reduce_scatter x1 -> x0, waiting for transfers between devices: 194 us -> none  [body(): lax.psum_scatter(jnp.dot(head_rows, out_proj, preferred_element_type=jnp....]
    ppermute x0 -> x16, waiting for transfers between devices: none -> 75.8 us  [the longest x9 64.2 us: swap_y(): return lax.ppermute(value, 'replica', SWAP_Y)]
    all_to_all x2 -> x0, blocking collectives: 43.9 us -> none  [the longest x1 22.7 us: body(): lax.all_to_all(outgoing, 'expert', split_axis=1, concat_axis=1, tiled=True)]
    all_to_all x1 -> x4, waiting for transfers between devices: 30.6 us -> 66.7 us  [the longest x1 27.8 us: body(): lax.all_to_all(outgoing, 'expert', split_axis=0, concat_axis=0, tiled=True)]
    all_to_all x1 -> x4, starting transfers between devices: 9.96 us -> 27.4 us  [the longest x2 12.5 us: same_x(): lax.all_to_all(value, 'expert', split_axis=0, concat_axis=0, axis_index_g...]
    ppermute x0 -> x16, starting transfers between devices: none -> 12 us  [the longest x9 6.84 us: swap_y(): return lax.ppermute(value, 'replica', SWAP_Y)]
    dot_general x5 -> x9, matrix products: 32.3 us -> 22.1 us  [the longest x2 7.51 us: partial(): jnp.dot(theirs, mats[1], preferred_element_type=f32)]
  transfers between devices with their start and end apart: 6 -> 20, of which waited for: 6 -> 12; matrix products, arithmetic and copies ran while one was open for 3% -> 18% of each run, Pallas kernels for 0% -> 0%
where the time goes in v1:
time: 235 us
  waiting for transfers between devices  143 us (61%)
  starting transfers between devices  39.3 us (17%)
  matrix products  33.1 us (14%)
  local copies, waits for them, and re-layouts  14.4 us (6%)
  other arithmetic  4.8 us (2%)
    ppermute x9, waiting for transfers between devices, swap_y(): return lax.ppermute(value, 'replica', SWAP_Y)  64.2 us
    all_to_all x1, waiting for transfers between devices, body(): lax.all_to_all(outgoing, 'expert', split_axis=0, concat_axis=0, tiled=True)  27.8 us
    all_to_all x2, waiting for transfers between devices, same_x(): lax.all_to_all(value, 'expert', split_axis=0, concat_axis=0, axis_index_g...  22.8 us
    all_to_all x1, waiting for transfers between devices, body(): lax.all_to_all(result, 'expert', split_axis=0, concat_axis=0, tiled=True)  16.1 us
    all_to_all x2, starting transfers between devices, same_x(): lax.all_to_all(value, 'expert', split_axis=0, concat_axis=0, axis_index_g...  12.5 us
    ppermute x3, waiting for transfers between devices, from_x(): return lax.ppermute(value, 'expert', pairs)  11.6 us
    dot_general x2, matrix products, partial(): jnp.dot(theirs, mats[1], preferred_element_type=f32)  7.51 us
    unnamed x25, local copies, waits for them, and re-layouts  7.49 us
  transfers between devices with their start and end apart: 20, of which 12 were waited for; matrix products, arithmetic and copies ran while one was open for 18% of the time, Pallas kernels for 0%

profile of v1, /device:TPU:0, one launch (start us, length us, event | category | flops | bytes accessed | tf_op | source)
XLA Modules:
  0.0 234.6 jit_solution(1317904733125492211)
XLA Ops:
  0.0 2.8 %collective-permute-start.2 = (bf16[256,1024]{1,0:T(8,128)(2,1)}, bf16[256,1024]{1,0:T(8,128)(2,1)}, u32[]{:S(2)}, u32[]{:S(2)}) collective-permute-start(bf16[256,1024]{1,0:T(8,128)(2,1)} %param.21), channel_id=1, source_target_pairs={{0,3},{1,0},{2,1},{3,2},{4,7},{5,4},{6,5},{7,6},{8,11},{9,8},{10,9... | collective-permute-start | bytes 1572872 | tf_op jit(solution)/shard_map/ppermute | solution.py:73
  2.8 0.8 collective-permute-start.3
  3.6 0.9 collective-permute-start.4
  4.5 0.7 iota_compare_fusion.2
  5.3 1.0 copy.61
  6.3 0.7 reshape.144
  7.0 5.8 %fusion.21 = (f32[16,4,16]{2,1,0:T(4,128)S(1)}, f32[16,4,16,512]{3,2,1,0:T(8,128)S(1)}) fusion(pred[16,512]{1,0:T(8,128)(4,1)S(1)} %iota_compare_fusion.2, bf16[16,4,16,128]{3,2,1,0:T(8,128)(2,1)S(1)} %bitcast.87, bf16[16,4,512,128]{3,2,1,0:T(8,128)(2,1)} %param.18), kind=kOutput, calls=%fused_computation.29 | convolution fusion | flops 135789568 | bytes 10760192 | tf_op jit(solution)/shard_map/rgqd,rgpd->rgqp/dot_general | solution.py:26
  13.1 0.9 constant_dynamic-update-slice_fusion.3
  14.0 11.6 %collective-permute-done.2 = bf16[256,1024]{1,0:T(8,128)(2,1)} collective-permute-done((bf16[256,1024]{1,0:T(8,128)(2,1)}, bf16[256,1024]{1,0:T(8,128)(2,1)}, u32[]{:S(2)}, u32[]{:S(2)}) %collective-permute-start.2) | collective-permute-done | bytes 524320 | tf_op jit(solution)/shard_map/ppermute | solution.py:73
  25.6 1.9 constant_dynamic-update-slice_fusion.2
  27.5 1.9 constant_dynamic-update-slice_fusion.1
  29.3 0.8 constant_dynamic-update-slice_fusion
  30.2 0.8 fusion.22
  31.0 4.9 %fusion.31 = bf16[16,4,16,128]{3,2,1,0:T(8,128)(2,1)S(1)} fusion(bf16[16,4,512,128]{3,2,1,0:T(8,128)(2,1)} %param.19, f32[16,4,16,512]{3,2,1,0:T(8,128)S(1)} %get-tuple-element.22, f32[16,4,16]{2,1,0:T(4,128)S(1)} %get-tuple-element.16, f32[16,4,16]{2,1,0:T(4,128)S(1)} %multiply_maximum_fusion, pred[16,512]{1,0:T(8,128)(4,1)S(1)} %iota_compare_fusion.2, ...), kind=kOutput, calls=%fused_computation.41 | convolution fusion | flops 137232384 | bytes 10801152 | tf_op jit(solution)/shard_map/rgqp,rgpd->rgqd/dot_general | solution.py:46
  36.8 0.9 copy.71
  37.6 8.0 %all-to-all-start = ((bf16[8,16,1024]{2,1,0:T(8,128)(2,1)}), bf16[8,16,1024]{2,1,0:T(8,128)(2,1)S(1)}, u32[]{:S(2)}, u32[]{:S(2)}) async-start(bf16[8,16,1024]{2,1,0:T(8,128)(2,1)} %bitcast.78), calls=%async_computation | async-start | bytes 524288 | tf_op jit(solution)/shard_map/all_to_all | solution.py:64
  45.6 9.2 %all-to-all-done = bf16[8,16,1024]{2,1,0:T(8,128)(2,1)S(1)} async-done(((bf16[8,16,1024]{2,1,0:T(8,128)(2,1)}), bf16[8,16,1024]{2,1,0:T(8,128)(2,1)S(1)}, u32[]{:S(2)}, u32[]{:S(2)}) %all-to-all-start) | async-done | bytes 262176 | tf_op jit(solution)/shard_map/all_to_all | solution.py:64
  54.9 0.7 collective-permute-start.1
  55.6 1.4 collective-permute-start
  57.7 4.7 %collective-permute-done.1 = bf16[8,16,1024]{2,1,0:T(8,128)(2,1)S(1)} collective-permute-done((bf16[8,16,1024]{2,1,0:T(8,128)(2,1)S(1)}, bf16[8,16,1024]{2,1,0:T(8,128)(2,1)S(1)}, u32[]{:S(2)}, u32[]{:S(2)}) %collective-permute-start.1) | collective-permute-done | bytes 262176 | tf_op jit(solution)/shard_map/ppermute | solution.py:56
  62.5 3.9 %fusion.15 = bf16[256,2048]{1,0:T(8,128)(2,1)} fusion(bf16[256,1024]{1,0:T(8,128)(2,1)S(1)} %bitcast.90, bf16[1024,1024]{1,0:T(8,128)(2,1)} %collective-permute-done.5, bf16[1024,1024]{1,0:T(8,128)(2,1)S(1)} %copy-done.1), kind=kOutput, calls=%fused_computation.18 | convolution fusion | flops 1082654720 | bytes 5767168 | tf_op jit(solution)/shard_map/dot_general | solution.py:145
  66.4 4.5 %all-to-all-start.1 = ((bf16[8,32,2048]{2,1,0:T(8,128)(2,1)}), bf16[8,32,2048]{2,1,0:T(8,128)(2,1)S(1)}, u32[]{:S(2)}, u32[]{:S(2)}) async-start(bf16[8,32,2048]{2,1,0:T(8,128)(2,1)} %bitcast.7), calls=%async_computation.1 | async-start | bytes 2097152 | tf_op jit(solution)/shard_map/all_to_all | solution.py:64
  72.0 13.5 %all-to-all-done.1 = bf16[8,32,2048]{2,1,0:T(8,128)(2,1)S(1)} async-done(((bf16[8,32,2048]{2,1,0:T(8,128)(2,1)}), bf16[8,32,2048]{2,1,0:T(8,128)(2,1)S(1)}, u32[]{:S(2)}, u32[]{:S(2)}) %all-to-all-start.1) | async-done | bytes 1048608 | tf_op jit(solution)/shard_map/all_to_all | solution.py:64
  85.8 0.8 collective-permute-start.8
  86.8 2.6 %collective-permute-done.8 = f32[32]{0:T(128)S(1)} collective-permute-done((f32[32]{0:T(128)S(1)}, f32[32]{0:T(128)S(1)}, u32[]{:S(2)}, u32[]{:S(2)}) %collective-permute-start.8) | collective-permute-done | bytes 160 | tf_op jit(solution)/shard_map/ppermute | solution.py:56
  89.7 0.8 fusion.14
  90.4 1.5 copy.70
  91.9 7.4 %all-to-all-start.2 = ((bf16[32,2,8,2048]{3,2,1,0:T(8,128)(2,1)}), bf16[32,2,8,2048]{3,2,1,0:T(8,128)(2,1)S(1)}, u32[]{:S(2)}, u32[]{:S(2)}) async-start(bf16[32,2,8,2048]{3,2,1,0:T(8,128)(2,1)} %bitcast.80), calls=%async_computation.2 | async-start | bytes 4194304 | tf_op jit(solution)/shard_map/all_to_all | solution.py:158
  99.9 27.8 %all-to-all-done.2 = bf16[32,2,8,2048]{3,2,1,0:T(8,128)(2,1)S(1)} async-done(((bf16[32,2,8,2048]{3,2,1,0:T(8,128)(2,1)}), bf16[32,2,8,2048]{3,2,1,0:T(8,128)(2,1)S(1)}, u32[]{:S(2)}, u32[]{:S(2)}) %all-to-all-start.2) | async-done | bytes 2097184 | tf_op jit(solution)/shard_map/all_to_all | solution.py:158
  127.9 1.7 copy-done.7
  129.6 1.8 fusion.12
  131.5 3.8 %convolution_add_fusion.1 = f32[512,1536]{1,0:T(8,128)S(1)} fusion(f32[512,1536]{1,0:T(8,128)S(1)} %fusion.12, bf16[1,1024,1536]{2,1,0:T(8,128)(2,1)} %collective-permute-done.9, bf16[512,2048]{1,0:T(8,128)(2,1)S(1)} %bitcast.84), kind=kOutput, calls=%fused_computation.5 | convolution fusion | flops 1611399168 | bytes 10485760 | tf_op jit(solution)/shard_map/dot_general | solution.py:163
  135.4 0.8 collective-permute-start.10
  136.2 1.8 fusion.9
  138.0 3.7 %convolution_add_fusion = f32[512,1536]{1,0:T(8,128)S(1)} fusion(f32[512,1536]{1,0:T(8,128)S(1)} %fusion.9, bf16[1,1024,1536]{2,1,0:T(8,128)(2,1)} %collective-permute-done.11, bf16[512,2048]{1,0:T(8,128)(2,1)S(1)} %bitcast.86), kind=kOutput, calls=%fused_computation.4 | convolution fusion | flops 1611399168 | bytes 10485760 | tf_op jit(solution)/shard_map/dot_general | solution.py:163
  141.8 1.4 collective-permute-start.12
  143.2 12.8 %collective-permute-done.10 = bf16[256,1536]{1,0:T(8,128)(2,1)S(1)} collective-permute-done((bf16[256,1536]{1,0:T(8,128)(2,1)S(1)}, bf16[256,1536]{1,0:T(8,128)(2,1)S(1)}, u32[]{:S(2)}, u32[]{:S(2)}) %collective-permute-start.10) | collective-permute-done | bytes 786464 | tf_op jit(solution)/shard_map/ppermute | solution.py:56
  155.9 13.6 %collective-permute-done.12 = bf16[256,1536]{1,0:T(8,128)(2,1)S(1)} collective-permute-done((bf16[256,1536]{1,0:T(8,128)(2,1)S(1)}, bf16[256,1536]{1,0:T(8,128)(2,1)S(1)}, u32[]{:S(2)}, u32[]{:S(2)}) %collective-permute-start.12) | collective-permute-done | bytes 786464 | tf_op jit(solution)/shard_map/ppermute | solution.py:56
  170.1 0.9 collective-permute-start.13
  171.0 15.4 %collective-permute-done.13 = bf16[256,1536]{1,0:T(8,128)(2,1)S(1)} collective-permute-done((bf16[256,1536]{1,0:T(8,128)(2,1)S(1)}, bf16[256,1536]{1,0:T(8,128)(2,1)S(1)}, u32[]{:S(2)}, u32[]{:S(2)}) %collective-permute-start.13) | collective-permute-done | bytes 786464 | tf_op jit(solution)/shard_map/ppermute | solution.py:56
  186.4 1.8 fusion.25
  188.3 3.7 %fusion.28 = bf16[512,1024]{1,0:T(8,128)(2,1)S(1)} fusion(bf16[1,1536,1024]{2,1,0:T(8,128)(2,1)} %collective-permute-done.14, bf16[256,1536]{1,0:T(8,128)(2,1)S(1)} %collective-permute-done.13, bf16[256,1536]{1,0:T(8,128)(2,1)S(1)} %fusion.24), kind=kOutput, calls=%fused_computation.39 | convolution fusion | flops 1614282752 | bytes 5767168 | tf_op jit(solution)/shard_map/dot_general | solution.py:174
  192.2 1.6 copy.69
  193.7 7.5 %all-to-all-start.3 = ((bf16[32,2,8,2048]{3,2,1,0:T(8,128)(2,1)}), bf16[32,2,8,2048]{3,2,1,0:T(8,128)(2,1)S(1)}, u32[]{:S(2)}, u32[]{:S(2)}) async-start(bf16[32,2,8,2048]{3,2,1,0:T(8,128)(2,1)} %bitcast.79), calls=%async_computation.3 | async-start | bytes 4194304 | tf_op jit(solution)/shard_map/all_to_all | solution.py:177
  201.3 10.9 %collective-permute-done.7 = f32[16,8]{0,1:T(8,128)S(1)} collective-permute-done((f32[16,8]{0,1:T(8,128)S(1)}, f32[16,8]{0,1:T(8,128)S(1)}, u32[]{:S(2)}, u32[]{:S(2)}) %collective-permute-start.7) | collective-permute-done | bytes 544 | tf_op jit(solution)/shard_map/ppermute | solution.py:56
  212.5 16.1 %all-to-all-done.3 = bf16[32,2,8,2048]{3,2,1,0:T(8,128)(2,1)S(1)} async-done(((bf16[32,2,8,2048]{3,2,1,0:T(8,128)(2,1)}), bf16[32,2,8,2048]{3,2,1,0:T(8,128)(2,1)S(1)}, u32[]{:S(2)}, u32[]{:S(2)}) %all-to-all-start.3) | async-done | bytes 2097184 | tf_op jit(solution)/shard_map/all_to_all | solution.py:177
  228.6 0.9 fusion.18
  229.6 4.3 %collective-permute-done.15 = bf16[16,2048]{1,0:T(8,128)(2,1)S(1)} collective-permute-done((bf16[16,2048]{1,0:T(8,128)(2,1)S(1)}, bf16[16,2048]{1,0:T(8,128)(2,1)S(1)}, u32[]{:S(2)}, u32[]{:S(2)}) %collective-permute-start.15) | collective-permute-done | bytes 65568 | tf_op jit(solution)/shard_map/ppermute | solution.py:56
  (78 shorter events, 6.6 us)
Async XLA Ops:
  0.0 25.6 %collective-permute-start.2 = (bf16[256,1024]{1,0:T(8,128)(2,1)}, bf16[256,1024]{1,0:T(8,128)(2,1)}, u32[]{:S(2)}, u32[]{:S(2)}) collective-permute-start(bf16[256,1024]{1,0:T(8,128)(2,1)} %param.21), channel_id=1, source_target_pairs={{0,3},{1,0},{2,1},{3,2},{4,7},{5,4},{6,5},{7,6},{8,11},{9,8},{10,9... | collective-permute-start | bytes 1572872 | tf_op jit(solution)/shard_map/ppermute | solution.py:73
  2.8 24.6 %collective-permute-start.3 = (bf16[256,1024]{1,0:T(8,128)(2,1)}, bf16[256,1024]{1,0:T(8,128)(2,1)}, u32[]{:S(2)}, u32[]{:S(2)}) collective-permute-start(bf16[256,1024]{1,0:T(8,128)(2,1)} %param.21), channel_id=1, source_target_pairs={{0,2},{1,3},{2,0},{3,1},{4,6},{5,7},{6,4},{7,5},{8,10},{9,11},{10,... | collective-permute-start | bytes 1572872 | tf_op jit(solution)/shard_map/ppermute | solution.py:73
  3.6 25.7 %collective-permute-start.4 = (bf16[256,1024]{1,0:T(8,128)(2,1)}, bf16[256,1024]{1,0:T(8,128)(2,1)S(1)}, u32[]{:S(2)}, u32[]{:S(2)}) collective-permute-start(bf16[256,1024]{1,0:T(8,128)(2,1)} %param.21), channel_id=1, source_target_pairs={{0,1},{1,2},{2,3},{3,0},{4,5},{5,6},{6,7},{7,4},{8,9},{9,10},{10,1... | collective-permute-start | bytes 1572872 | tf_op jit(solution)/shard_map/ppermute | solution.py:73
  7.0 6.1 %copy-start = (bf16[256,1024]{1,0:T(8,128)(2,1)S(1)}, bf16[256,1024]{1,0:T(8,128)(2,1)}, u32[]{:S(2)}) copy-start(bf16[256,1024]{1,0:T(8,128)(2,1)} %param.21) | copy-start | bytes 1572868
  7.0 7.0 %copy-start.3 = (bf16[16,512]{1,0:T(8,128)(2,1)S(1)}, bf16[16,512]{1,0:T(8,128)(2,1)}, u32[]{:S(2)}) copy-start(bf16[16,512]{1,0:T(8,128)(2,1)} %param.17) | copy-start | bytes 49156
  30.2 32.3 %collective-permute-start.5 = (bf16[1024,1024]{1,0:T(8,128)(2,1)}, bf16[1024,1024]{1,0:T(8,128)(2,1)}, u32[]{:S(2)}, u32[]{:S(2)}) collective-permute-start(bf16[1024,1024]{1,0:T(8,128)(2,1)} %constant_dynamic-update-slice_fusion), channel_id=1, source_target_pairs={{0,32},{32,0},{64,96},{96,64},{1,33},{33,1},{65,97},{97,65},{2,34}... | collective-permute-start | bytes 6291464 | tf_op jit(solution)/shard_map/ppermute | solution.py:60
  35.9 19.6 %copy-start.2 = (bf16[16,4096]{1,0:T(8,128)(2,1)S(1)}, bf16[16,4096]{1,0:T(8,128)(2,1)}, u32[]{:S(2)}) copy-start(bf16[16,4096]{1,0:T(8,128)(2,1)} %param.14) | copy-start | bytes 393220
  35.9 21.1 %copy-start.5 = (s32[16,8]{0,1:T(8,128)S(1)}, s32[16,8]{0,1:T(8,128)}, u32[]{:S(2)}) copy-start(s32[16,8]{0,1:T(8,128)} %param.23) | copy-start | bytes 1540
  36.1 26.4 %copy-start.1 = (bf16[1024,1024]{1,0:T(8,128)(2,1)S(1)}, bf16[1024,1024]{1,0:T(8,128)(2,1)}, u32[]{:S(2)}) copy-start(bf16[1024,1024]{1,0:T(8,128)(2,1)} %constant_dynamic-update-slice_fusion) | copy-start | bytes 6291460
  37.6 17.2 %all-to-all-start = ((bf16[8,16,1024]{2,1,0:T(8,128)(2,1)}), bf16[8,16,1024]{2,1,0:T(8,128)(2,1)S(1)}, u32[]{:S(2)}, u32[]{:S(2)}) async-start(bf16[8,16,1024]{2,1,0:T(8,128)(2,1)} %bitcast.78), calls=%async_computation | async-start | bytes 524288 | tf_op jit(solution)/shard_map/all_to_all | solution.py:64
  54.9 7.6 %collective-permute-start.1 = (bf16[8,16,1024]{2,1,0:T(8,128)(2,1)S(1)}, bf16[8,16,1024]{2,1,0:T(8,128)(2,1)S(1)}, u32[]{:S(2)}, u32[]{:S(2)}) collective-permute-start(bf16[8,16,1024]{2,1,0:T(8,128)(2,1)S(1)} %all-to-all-done), channel_id=1, source_target_pairs={{0,64},{32,96},{64,0},{96,32},{1,65},{33,97},{65,1},{97,33},{2,66}... | collective-permute-start | bytes 786440 | tf_op jit(solution)/shard_map/ppermute | solution.py:56
  55.6 30.1 %collective-permute-start = (bf16[16,2048]{1,0:T(8,128)(2,1)S(1)}, bf16[16,2048]{1,0:T(8,128)(2,1)S(1)}, u32[]{:S(2)}, u32[]{:S(2)}) collective-permute-start(bf16[16,2048]{1,0:T(8,128)(2,1)S(1)} %pad_maximum_fusion.6), channel_id=1, source_target_pairs={{0,64},{32,96},{64,0},{96,32},{1,65},{33,97},{65,1},{97,33},{2,66}... | collective-permute-start | bytes 196616 | tf_op jit(solution)/shard_map/ppermute | solution.py:56
  57.0 14.1 %collective-permute-start.6 = (s32[16,8]{0,1:T(8,128)S(1)}, s32[16,8]{0,1:T(8,128)S(1)}, u32[]{:S(2)}, u32[]{:S(2)}) collective-permute-start(s32[16,8]{0,1:T(8,128)S(1)} %copy-done.5), channel_id=1, source_target_pairs={{0,64},{32,96},{64,0},{96,32},{1,65},{33,97},{65,1},{97,33},{2,66}... | collective-permute-start | bytes 1544 | tf_op jit(solution)/shard_map/ppermute | solution.py:56
  57.7 73.8 %collective-permute-start.9 = (bf16[1,1024,1536]{2,1,0:T(8,128)(2,1)}, bf16[1,1024,1536]{2,1,0:T(8,128)(2,1)}, u32[]{:S(2)}, u32[]{:S(2)}) collective-permute-start(bf16[1,1024,1536]{2,1,0:T(8,128)(2,1)} %param.25), channel_id=1, source_target_pairs={{0,32},{32,0},{64,96},{96,64},{1,33},{33,1},{65,97},{97,65},{2,34}... | collective-permute-start | bytes 9437192 | tf_op jit(solution)/shard_map/ppermute | solution.py:60
  66.4 4.5 %copy-start.4 = (f32[4096]{0:T(1024)S(1)}, f32[4096]{0:T(1024)}, u32[]{:S(2)}) copy-start(f32[4096]{0:T(1024)} %param.22) | copy-start | bytes 49156
  66.4 19.1 %all-to-all-start.1 = ((bf16[8,32,2048]{2,1,0:T(8,128)(2,1)}), bf16[8,32,2048]{2,1,0:T(8,128)(2,1)S(1)}, u32[]{:S(2)}, u32[]{:S(2)}) async-start(bf16[8,32,2048]{2,1,0:T(8,128)(2,1)} %bitcast.7), calls=%async_computation.1 | async-start | bytes 2097152 | tf_op jit(solution)/shard_map/all_to_all | solution.py:64
  85.8 3.6 %collective-permute-start.8 = (f32[32]{0:T(128)S(1)}, f32[32]{0:T(128)S(1)}, u32[]{:S(2)}, u32[]{:S(2)}) collective-permute-start(f32[32]{0:T(128)S(1)} %get-tuple-element.5), channel_id=1, source_target_pairs={{0,64},{32,96},{64,0},{96,32},{1,65},{33,97},{65,1},{97,33},{2,66}... | collective-permute-start | bytes 392 | tf_op jit(solution)/shard_map/ppermute | solution.py:56
  91.9 35.9 %all-to-all-start.2 = ((bf16[32,2,8,2048]{3,2,1,0:T(8,128)(2,1)}), bf16[32,2,8,2048]{3,2,1,0:T(8,128)(2,1)S(1)}, u32[]{:S(2)}, u32[]{:S(2)}) async-start(bf16[32,2,8,2048]{3,2,1,0:T(8,128)(2,1)} %bitcast.80), calls=%async_computation.2 | async-start | bytes 4194304 | tf_op jit(solution)/shard_map/all_to_all | solution.py:158
  99.3 38.7 %collective-permute-start.11 = (bf16[1,1024,1536]{2,1,0:T(8,128)(2,1)}, bf16[1,1024,1536]{2,1,0:T(8,128)(2,1)}, u32[]{:S(2)}, u32[]{:S(2)}) collective-permute-start(bf16[1,1024,1536]{2,1,0:T(8,128)(2,1)} %param.26), channel_id=1, source_target_pairs={{0,32},{32,0},{64,96},{96,64},{1,33},{33,1},{65,97},{97,65},{2,34}... | collective-permute-start | bytes 9437192 | tf_op jit(solution)/shard_map/ppermute | solution.py:60
  99.4 88.8 %collective-permute-start.14 = (bf16[1,1536,1024]{2,1,0:T(8,128)(2,1)}, bf16[1,1536,1024]{2,1,0:T(8,128)(2,1)}, u32[]{:S(2)}, u32[]{:S(2)}) collective-permute-start(bf16[1,1536,1024]{2,1,0:T(8,128)(2,1)} %param.27), channel_id=1, source_target_pairs={{0,32},{32,0},{64,96},{96,64},{1,33},{33,1},{65,97},{97,65},{2,34}... | collective-permute-start | bytes 9437192 | tf_op jit(solution)/shard_map/ppermute | solution.py:60
  127.8 1.9 copy-start.7
  131.4 4.8 %copy-start.8 = (bf16[1,1024,1536]{2,1,0:T(8,128)(2,1)S(1)}, bf16[1,1024,1536]{2,1,0:T(8,128)(2,1)}, u32[]{:S(2)}) copy-start(bf16[1,1024,1536]{2,1,0:T(8,128)(2,1)} %param.26) | copy-start | bytes 9437188
  135.4 20.6 %collective-permute-start.10 = (bf16[256,1536]{1,0:T(8,128)(2,1)S(1)}, bf16[256,1536]{1,0:T(8,128)(2,1)S(1)}, u32[]{:S(2)}, u32[]{:S(2)}) collective-permute-start(bf16[256,1536]{1,0:T(8,128)(2,1)S(1)} %slice.209), channel_id=1, source_target_pairs={{0,64},{32,96},{64,0},{96,32},{1,65},{33,97},{65,1},{97,33},{2,66}... | collective-permute-start | bytes 2359304 | tf_op jit(solution)/shard_map/ppermute | solution.py:56
  141.8 44.7 %copy-start.9 = (bf16[1,1536,1024]{2,1,0:T(8,128)(2,1)S(1)}, bf16[1,1536,1024]{2,1,0:T(8,128)(2,1)}, u32[]{:S(2)}) copy-start(bf16[1,1536,1024]{2,1,0:T(8,128)(2,1)} %param.27) | copy-start | bytes 9437188
  141.8 27.7 %collective-permute-start.12 = (bf16[256,1536]{1,0:T(8,128)(2,1)S(1)}, bf16[256,1536]{1,0:T(8,128)(2,1)S(1)}, u32[]{:S(2)}, u32[]{:S(2)}) collective-permute-start(bf16[256,1536]{1,0:T(8,128)(2,1)S(1)} %slice.208), channel_id=1, source_target_pairs={{0,64},{32,96},{64,0},{96,32},{1,65},{33,97},{65,1},{97,33},{2,66}... | collective-permute-start | bytes 2359304 | tf_op jit(solution)/shard_map/ppermute | solution.py:56
  170.1 16.3 %collective-permute-start.13 = (bf16[256,1536]{1,0:T(8,128)(2,1)S(1)}, bf16[256,1536]{1,0:T(8,128)(2,1)S(1)}, u32[]{:S(2)}, u32[]{:S(2)}) collective-permute-start(bf16[256,1536]{1,0:T(8,128)(2,1)S(1)} %fusion.24), channel_id=1, source_target_pairs={{0,64},{32,96},{64,0},{96,32},{1,65},{33,97},{65,1},{97,33},{2,66}... | collective-permute-start | bytes 2359304 | tf_op jit(solution)/shard_map/ppermute | solution.py:56
  193.7 7.5 %copy-start.6 = (f32[16,8]{0,1:T(8,128)S(1)}, f32[16,8]{0,1:T(8,128)}, u32[]{:S(2)}) copy-start(f32[16,8]{0,1:T(8,128)} %param.24) | copy-start | bytes 1540
  193.7 34.8 %all-to-all-start.3 = ((bf16[32,2,8,2048]{3,2,1,0:T(8,128)(2,1)}), bf16[32,2,8,2048]{3,2,1,0:T(8,128)(2,1)S(1)}, u32[]{:S(2)}, u32[]{:S(2)}) async-start(bf16[32,2,8,2048]{3,2,1,0:T(8,128)(2,1)} %bitcast.79), calls=%async_computation.3 | async-start | bytes 4194304 | tf_op jit(solution)/shard_map/all_to_all | solution.py:177
  201.2 11.0 %collective-permute-start.7 = (f32[16,8]{0,1:T(8,128)S(1)}, f32[16,8]{0,1:T(8,128)S(1)}, u32[]{:S(2)}, u32[]{:S(2)}) collective-permute-start(f32[16,8]{0,1:T(8,128)S(1)} %copy-done.6), channel_id=1, source_target_pairs={{0,64},{32,96},{64,0},{96,32},{1,65},{33,97},{65,1},{97,33},{2,66}... | collective-permute-start | bytes 1544 | tf_op jit(solution)/shard_map/ppermute | solution.py:56
  229.6 4.3 %collective-permute-start.15 = (bf16[16,2048]{1,0:T(8,128)(2,1)S(1)}, bf16[16,2048]{1,0:T(8,128)(2,1)S(1)}, u32[]{:S(2)}, u32[]{:S(2)}) collective-permute-start(bf16[16,2048]{1,0:T(8,128)(2,1)S(1)} %slice.97), channel_id=1, source_target_pairs={{0,64},{32,96},{64,0},{96,32},{1,65},{33,97},{65,1},{97,33},{2,66}... | collective-permute-start | bytes 196616 | tf_op jit(solution)/shard_map/ppermute | solution.py:56

commit v2 on v1

--- a/solution.py
+++ b/solution.py
@@ -1,7 +1,11 @@
 import jax
 import jax.numpy as jnp
 from jax import lax
+from jax.experimental import pallas as pl
+from jax.experimental.pallas import tpu as pltpu
 from jax.sharding import PartitionSpec as P
+
+MESH = pl.DeviceIdType.MESH
 
 HD = 128
 TOP = 8
@@ -60,6 +64,10 @@
     return lax.ppermute(value, "replica", SWAP_CORE)
 
 
+def swap_plane(value):
+    return lax.ppermute(value, "expert", [(e, (e + 16) % EXPERTS) for e in range(EXPERTS)])
+
+
 def same_x(value):
     return lax.all_to_all(
         value, "expert", split_axis=0, concat_axis=0, axis_index_groups=SAME_X, tiled=True
@@ -88,6 +96,350 @@
         jnp.where(chip == 0, c, a),
         jnp.where(chip == 0, d, b),
     )
+
+
+def offset(s):
+    dz = s % 8 // 2
+    return dz, 2 * (s % 2) + (dz + s // 8) % 2
+
+
+def shifted(expert, s, sign):
+    dz, dx = offset(s)
+    plane, z, x = expert // 16, expert // 4 % 4, expert % 4
+    return plane * 16 + (z + 4 + sign * dz) % 4 * 4 + (x + 4 + sign * dx) % 4
+
+
+def moe_kernel(
+    mid_ref,
+    gain_ref,
+    placing_ref,
+    weighting_ref,
+    wg0,
+    wg1,
+    wu0,
+    wu1,
+    wd0,
+    wd1,
+    out_ref,
+    v_gate,
+    v_up,
+    v_down,
+    square_out,
+    square_in,
+    scaled,
+    scaled_in,
+    rows_all,
+    outgoing,
+    block,
+    part_out,
+    part_in,
+    part_own,
+    units,
+    result,
+    returned,
+    mixed,
+    last_out,
+    last_bf,
+    last_in,
+    last_bf_in,
+    w_sem,
+    pre_send,
+    pre_recv,
+    disp_send,
+    disp_recv,
+    part_send,
+    part_recv,
+    unit_send,
+    unit_recv,
+    ret_send,
+    ret_recv,
+    last_send,
+    last_recv,
+):
+    f32, bf16 = jnp.float32, jnp.bfloat16
+    replica, expert = lax.axis_index("replica"), lax.axis_index("expert")
+    other_replica, other_plane = (replica + 2) % 4, (expert + 16) % 32
+    beside = (other_replica, expert)
+    across = (replica, other_plane)
+    diagonal = (other_replica, other_plane)
+    tile = 512
+    hidden = v_gate.shape[2]
+    quarter = v_gate.shape[1]
+    half = 2 * quarter
+
+    loads = [
+        pltpu.make_async_copy(src, dst, w_sem.at[i])
+        for i, (src, dst) in enumerate(
+            [
+                (wg0, v_gate.at[0]),
+                (wg1, v_gate.at[1]),
+                (wu0, v_up.at[0]),
+                (wu1, v_up.at[1]),
+                (wd0, v_down.at[0]),
+                (wd1, v_down.at[1]),
+            ]
+        )
+    ]
+    for load in loads:
+        load.start()
+
+    barrier = pltpu.get_barrier_semaphore()
+
+    @pl.loop(1, 16)
+    def _(s):
+        pl.semaphore_signal(
+            barrier, inc=1, device_id=(replica, shifted(expert, s, 1)), device_id_type=MESH
+        )
+
+    for device in (beside, across, diagonal):
+        pl.semaphore_signal(barrier, inc=1, device_id=device, device_id_type=MESH)
+    pl.semaphore_wait(barrier, 18)
+
+    def remote(src, dst, send, recv, device):
+        return pltpu.make_async_remote_copy(
+            src_ref=src,
+            dst_ref=dst,
+            send_sem=send,
+            recv_sem=recv,
+            device_id=device,
+            device_id_type=MESH,
+        )
+
+    mid = mid_ref[...]
+    square_out[...] = jnp.broadcast_to(jnp.sum(mid * mid, axis=-1, keepdims=True), (32, 128))
+    scaled[...] = (mid * gain_ref[...]).astype(bf16)
+    pre = [
+        remote(square_out, square_in.at[i], pre_send.at[i], pre_recv.at[i], device)
+        for i, device in enumerate((beside, across, diagonal))
+    ]
+    pre.append(remote(scaled, scaled_in, pre_send.at[3], pre_recv.at[3], across))
+    for copy in (pre[3], pre[0], pre[1], pre[2]):
+        copy.start()
+    for copy in pre:
+        copy.wait_recv()
+    for h in range(2):
+        here, there = pl.ds(16 * h, 16), pl.ds(16 * (1 - h), 16)
+        width = 2.0 * half
+        total = square_out[here, :1] + square_in[0, there, :1]
+        normed = mid_ref[here, :] * gain_ref[...] * lax.rsqrt(total / width + 1e-06)
+        rows_all[h, :16, :] = normed.astype(bf16)
+        total = square_in[1, here, :1] + square_in[2, there, :1]
+        normed = scaled_in[here, :].astype(f32) * lax.rsqrt(total / width + 1e-06)
+        rows_all[h, 16:, :] = normed.astype(bf16)
+
+    def dispatch(h, s):
+        rows = pl.ds(pl.multiple_of(s * 16, 16), 16)
+        return remote(
+            outgoing.at[h, rows],
+            block.at[h, rows],
+            disp_send.at[h, s],
+            disp_recv.at[h, s],
+            (replica, shifted(expert, s, 1)),
+        )
+
+    for h in (1, 0):
+
+        @pl.loop(0, half // tile)
+        def _(n):
+            cols = pl.ds(pl.multiple_of(n * tile, tile), tile)
+            outgoing[h, :, cols] = jnp.dot(
+                placing_ref[h], rows_all[h, :, cols], preferred_element_type=f32
+            ).astype(bf16)
+
+        @pl.loop(1, 16)
+        def _(s):
+            dispatch(h, s).start()
+
+        block[h, :16, :] = outgoing[h, :16, :]
+
+    def gate_up(h, start, count, store):
+        rows = pl.ds(start, count)
+
+        @pl.loop(0, hidden // tile)
+        def _(n):
+            at = pl.multiple_of(n * tile, tile)
+            for which, mats in enumerate((v_gate, v_up)):
+                value = jnp.dot(
+                    block[h, rows, :quarter],
+                    mats[0, :, pl.ds(at, tile)],
+                    preferred_element_type=f32,
+                ) + jnp.dot(
+                    block[h, rows, quarter:],
+                    mats[1, :, pl.ds(at, tile)],
+                    preferred_element_type=f32,
+                )
+                store(which, pl.ds(at, tile), value)
+
+    parts = [
+        remote(part_out.at[c], part_in.at[c], part_send.at[c], part_recv.at[c], beside)
+        for c in range(2)
+    ]
+    for load in loads[:4]:
+        load.wait()
+    for c in range(2):
+
+        @pl.loop(max(1, 8 * c), 8 * c + 8)
+        def _(s):
+            dispatch(1, s).wait_recv()
+
+        def store_out(which, cols, value):
+            part_out[c, which, :, cols] = value.astype(bf16)
+
+        gate_up(1, 128 * c, 128, store_out)
+        parts[c].start()
+
+    @pl.loop(1, 16)
+    def _(s):
+        dispatch(0, s).wait_recv()
+
+    def store_own(which, cols, value):
+        part_own[which, :, cols] = value
+
+    gate_up(0, 0, 256, store_own)
+
+    def give_back(h, s):
+        rows = pl.ds(pl.multiple_of(s * 16, 16), 16)
+        return remote(
+            result.at[h, rows],
+            returned.at[h, rows],
+            ret_send.at[h, s],
+            ret_recv.at[h, s],
+            (replica, shifted(expert, s, -1)),
+        )
+
+    def down(h, c):
+        for q in range(2):
+
+            @pl.loop(0, quarter // tile)
+            def _(n):
+                at = pl.multiple_of(n * tile, tile)
+                result[h, pl.ds(128 * c, 128), pl.ds(q * quarter + at, tile)] = jnp.dot(
+                    units[h, c], v_down[q, :, pl.ds(at, tile)], preferred_element_type=f32
+                ).astype(bf16)
+
+        @pl.loop(max(1, 8 * c), 8 * c + 8)
+        def _(s):
+            give_back(h, s).start()
+
+        if c == 0:
+            returned[h, :16, :] = result[h, :16, :]
+
+    sends = [
+        remote(units.at[0, c], units.at[1, c], unit_send.at[c], unit_recv.at[c], beside)
+        for c in range(2)
+    ]
+    for c in range(2):
+        parts[c].wait_recv()
+
+        @pl.loop(0, hidden // tile)
+        def _(n):
+            cols = pl.ds(pl.multiple_of(n * tile, tile), tile)
+            rows = pl.ds(128 * c, 128)
+            gate = part_own[0, rows, cols] + part_in[c, 0, :, cols].astype(f32)
+            up_val = part_own[1, rows, cols] + part_in[c, 1, :, cols].astype(f32)
+            units[0, c, :, cols] = (gate / (1.0 + jnp.exp(-gate)) * up_val).astype(bf16)
+
+        sends[c].start()
+        if c == 0:
+            loads[4].wait()
+            loads[5].wait()
+        down(0, c)
+    for c in range(2):
+        sends[c].wait_recv()
+        down(1, c)
+
+    for h in range(2):
+
+        @pl.loop(1, 16)
+        def _(s):
+            give_back(h, s).wait_recv()
+
+    @pl.loop(0, half // tile)
+    def _(n):
+        cols = pl.ds(pl.multiple_of(n * tile, tile), tile)
+        for h in range(2):
+            three = jnp.dot(weighting_ref[h], returned[h, :, cols], preferred_element_type=f32)
+            mixed[h, :, cols] = three[:32] + three[32:64] + three[64:]
+
+    last_out[...] = mid_ref[16:, :] + mixed[1, :16, :]
+    last_bf[0] = mixed[0, 16:, :].astype(bf16)
+    last_bf[1] = mixed[1, 16:, :].astype(bf16)
+    last = [
+        remote(last_out, last_in, last_send.at[0], last_recv.at[0], beside),
+        remote(last_bf.at[0], last_bf_in.at[0], last_send.at[1], last_recv.at[1], across),
+        remote(last_bf.at[1], last_bf_in.at[1], last_send.at[2], last_recv.at[2], diagonal),
+    ]
+    for copy in last:
+        copy.start()
+    for copy in last:
+        copy.wait_recv()
+    out_ref[0] = (mid_ref[:16, :] + mixed[0, :16, :] + last_bf_in[0].astype(f32)).astype(bf16)
+    out_ref[1] = (last_in[...] + last_bf_in[1].astype(f32)).astype(bf16)
+
+    for copy in pre + parts + sends + last:
+        copy.wait_send()
+    for h in range(2):
+
+        @pl.loop(1, 16)
+        def _(s):
+            dispatch(h, s).wait_send()
+            give_back(h, s).wait_send()
+
+
+def moe(mid, gain, placing, weighting, gate_mats, up_mats, down_mats):
+    f32, bf16 = jnp.float32, jnp.bfloat16
+    quarter, hidden = gate_mats[0].shape
+    half = 2 * quarter
+    vmem, anywhere = pl.BlockSpec(memory_space=pltpu.VMEM), pl.BlockSpec(memory_space=pl.ANY)
+    dma = pltpu.SemaphoreType.DMA
+    return pl.pallas_call(
+        moe_kernel,
+        out_shape=jax.ShapeDtypeStruct((2, 16, half), bf16),
+        in_specs=[vmem] * 4 + [anywhere] * 6,
+        out_specs=vmem,
+        scratch_shapes=[
+            pltpu.VMEM((2, quarter, hidden), bf16),
+            pltpu.VMEM((2, quarter, hidden), bf16),
+            pltpu.VMEM((2, hidden, quarter), bf16),
+            pltpu.VMEM((32, 128), f32),
+            pltpu.VMEM((3, 32, 128), f32),
+            pltpu.VMEM((32, half), bf16),
+            pltpu.VMEM((32, half), bf16),
+            pltpu.VMEM((2, 32, half), bf16),
+            pltpu.VMEM((2, 256, half), bf16),
+            pltpu.VMEM((2, 256, half), bf16),
+            pltpu.VMEM((2, 2, 128, hidden), bf16),
+            pltpu.VMEM((2, 2, 128, hidden), bf16),
+            pltpu.VMEM((2, 256, hidden), f32),
+            pltpu.VMEM((2, 2, 128, hidden), bf16),
+            pltpu.VMEM((2, 256, half), bf16),
+            pltpu.VMEM((2, 256, half), bf16),
+            pltpu.VMEM((2, 32, half), f32),
+            pltpu.VMEM((16, half), f32),
+            pltpu.VMEM((2, 16, half), bf16),
+            pltpu.VMEM((16, half), f32),
+            pltpu.VMEM((2, 16, half), bf16),
+            dma((6,)),
+            dma((4,)),
+            dma((4,)),
+            dma((2, 16)),
+            dma((2, 16)),
+            dma((2,)),
+            dma((2,)),
+            dma((2,)),
+            dma((2,)),
+            dma((2, 16)),
+            dma((2, 16)),
+            dma((3,)),
+            dma((3,)),
+        ],
+        compiler_params=pltpu.CompilerParams(
+            collective_id=0, has_side_effects=True, vmem_limit_bytes=50 * 1024 * 1024
+        ),
+        cost_estimate=pl.CostEstimate(
+            flops=10 * 10**9, bytes_accessed=20 * 10**6, transcendentals=10**6
+        ),
+    )(mid, gain, placing, weighting, *gate_mats, *up_mats, *down_mats)
 
 
 def body(
@@ -126,15 +478,26 @@
     gain = relative([norm_gain[q * quarter : (q + 1) * quarter] for q in range(4)], replica)
     gain = jnp.concatenate(gain[:2])
 
-    route2 = jnp.stack([routes, swap_y(routes)])
-    weight2 = jnp.stack([gate_weights, swap_y(gate_weights)])
-    flat = route2.reshape(2, rows * TOP)
-    onehot = (flat[:, :, None] == jnp.arange(EXPERTS)[None, None, :]).astype(jnp.int32)
-    rank = jnp.sum((jnp.cumsum(onehot, axis=1) - 1) * onehot, axis=2)
-    target = (flat * CAP + rank).reshape(2, rows, TOP)
-    chosen = target[..., None] == jnp.arange(EXPERTS * CAP)
-    placing = jnp.any(chosen, axis=2).astype(bf16)
-    weighting = jnp.sum(jnp.where(chosen, weight2[..., None], 0.0), axis=2)
+    expert = lax.axis_index("expert")
+
+    def of_four(value):
+        value = jnp.stack([value, swap_y(value)])
+        return jnp.stack([value, swap_plane(value)], axis=1)
+
+    route4, weight4 = of_four(routes), of_four(gate_weights)
+    flat = route4.reshape(2, 2, rows * TOP)
+    onehot = (flat[..., None] == jnp.arange(EXPERTS)).astype(jnp.int32)
+    rank = jnp.sum((jnp.cumsum(onehot, axis=2) - 1) * onehot, axis=3).reshape(route4.shape)
+    dz, dx = (route4 // 4 - expert // 4) % 4, (route4 - expert) % 4
+    place = ((dz + dx) % 2 * 8 + dz * 2 + dx // 2) * 16 + rank
+    place = place + CAP * jnp.arange(2)[None, :, None, None]
+    place = jnp.where(route4 // 16 == expert // 16, place, -1).reshape(2, 2 * rows, TOP)
+    chosen = place[..., None] == jnp.arange(EXPERTS * CAP)
+    placing = jnp.any(chosen, axis=2).astype(bf16).transpose(0, 2, 1)
+    weighting = jnp.sum(jnp.where(chosen, weight4.reshape(2, 2 * rows, TOP, 1), 0.0), axis=2)
+    high = lax.reduce_precision(weighting, 8, 7)
+    middle = lax.reduce_precision(weighting - high, 8, 7)
+    weighting = jnp.concatenate([high, middle, weighting - high - middle], axis=1).astype(bf16)
 
     attn = attend_local(query, key_new, value_new, key_cache, value_cache, cache_len)
     heads = attn.reshape(rows, GROUPS, LINE, -1)
@@ -146,42 +509,7 @@
     part = same_x(part.astype(bf16).reshape(GROUPS, 2 * rows, 2 * quarter))
     mid = hid + jnp.sum(part.astype(f32), axis=0)
 
-    squares = jnp.sum(mid * mid, axis=-1)
-    there = swap_y(squares)
-    squares = squares + jnp.concatenate([there[rows:], there[:rows]])
-    normed = (mid * lax.rsqrt(squares / width + 1e-06)[:, None] * gain).astype(bf16)
-
-    outgoing = jnp.einsum(
-        "hrs,hrd->hsd", placing, normed.reshape(2, rows, 2 * quarter), preferred_element_type=f32
-    ).astype(bf16)
-    outgoing = outgoing.reshape(2, EXPERTS, CAP, 2 * quarter).transpose(1, 0, 2, 3)
-    block = lax.all_to_all(outgoing, "expert", split_axis=0, concat_axis=0, tiled=True)
-    block = block.transpose(1, 0, 2, 3).reshape(2 * EXPERTS * CAP, 2 * quarter)
-    ours, theirs = block[:, :quarter], block[:, quarter:]
-
-    def partial(mats):
-        return jnp.dot(ours, mats[0], preferred_element_type=f32) + jnp.dot(
-            theirs, mats[1], preferred_element_type=f32
-        )
-
-    half = EXPERTS * CAP
-    gate, up_val = partial(gate_mats), partial(up_mats)
-    gate = gate[:half] + swap_y(gate[half:].astype(bf16)).astype(f32)
-    up_val = up_val[:half] + swap_y(up_val[half:].astype(bf16)).astype(f32)
-    units = (jax.nn.silu(gate) * up_val).astype(bf16)
-    units = jnp.concatenate([units, swap_y(units)], axis=0)
-    result = jnp.concatenate(
-        [jnp.dot(units, mat, preferred_element_type=f32).astype(bf16) for mat in down_mats], axis=1
-    )
-    result = result.reshape(2, EXPERTS, CAP, 2 * quarter).transpose(1, 0, 2, 3)
-    returned = lax.all_to_all(result, "expert", split_axis=0, concat_axis=0, tiled=True)
-    returned = returned.transpose(1, 0, 2, 3).reshape(2, EXPERTS * CAP, 2 * quarter)
-    mixture = jnp.einsum(
-        "hrs,hsd->hrd", weighting, returned.astype(f32), precision=lax.Precision.HIGHEST
-    )
-    out = (mid + mixture.reshape(2 * rows, 2 * quarter)).astype(bf16)
-    there = swap_y(out[rows:])
-    here = out[:rows]
+    here, there = moe(mid, gain[None, :], placing, weighting, gate_mats, up_mats, down_mats)
     return jnp.concatenate(
         relative(
             (here[:, :quarter], here[:, quarter:], there[:, :quarter], there[:, quarter:]), replica

time: 235 us -> 188 us (0.80)
  waiting for transfers between devices: 143 us -> 27.9 us
  Pallas kernels: 0 us -> 83.3 us
  matrix products: 33.1 us -> 16.2 us
  other arithmetic: 4.8 us -> 12.3 us
  starting transfers between devices: 39.3 us -> 32.6 us
    pallas_call x0 -> x1, Pallas kernels: none -> 83.3 us  [moe(): pl.pallas_call(moe_kernel, out_shape=jax.ShapeDtypeStruct((2, 16, half),...]
    ppermute x9 -> x4, waiting for transfers between devices: 64.2 us -> 6.35 us  [swap_y(): return lax.ppermute(value, 'replica', SWAP_Y)]
    all_to_all x2 -> x0, waiting for transfers between devices: 43.9 us -> none  [the longest x1 27.8 us: body(): lax.all_to_all(outgoing, 'expert', split_axis=0, concat_axis=0, tiled=True)]
    dot_general x8 -> x0, matrix products: 18.3 us -> none  [the longest x2 7.51 us: partial(): jnp.dot(theirs, mats[1], preferred_element_type=f32)]
    all_to_all x2 -> x0, starting transfers between devices: 14.9 us -> none  [the longest x1 7.48 us: body(): lax.all_to_all(result, 'expert', split_axis=0, concat_axis=0, tiled=True)]
    all_to_all x2, waiting for transfers between devices: 22.8 us -> 10.8 us  [same_x(): lax.all_to_all(value, 'expert', split_axis=0, concat_axis=0, axis_index_g...]
    ppermute x0 -> x2, starting transfers between devices: none -> 6.62 us  [swap_plane(): lax.ppermute(value, 'expert', [(e, (e + 16) % EXPERTS) for e in range(EXP...]
    all_to_all x2, starting transfers between devices: 12.5 us -> 16.3 us  [same_x(): lax.all_to_all(value, 'expert', split_axis=0, concat_axis=0, axis_index_g...]
  transfers between devices with their start and end apart: 20 -> 15, of which waited for: 12 -> 6; matrix products, arithmetic and copies ran while one was open for 18% -> 22% of each run, Pallas kernels for 0% -> 0%
where the time goes in v2:
time: 188 us; the launch traced here: 187 us
  Pallas kernels  83.3 us (44%)
  starting transfers between devices  32.6 us (17%)
  waiting for transfers between devices  27.9 us (15%)
  matrix products  16.2 us (9%)
  local copies, waits for them, and re-layouts  14.2 us (8%)
  other arithmetic  12.3 us (7%)
    pallas_call x1, Pallas kernels, moe(): pl.pallas_call(moe_kernel, out_shape=jax.ShapeDtypeStruct((2, 16, half),...  83.3 us
    all_to_all x2, starting transfers between devices, same_x(): lax.all_to_all(value, 'expert', split_axis=0, concat_axis=0, axis_index_g...  16.3 us
    all_to_all x2, waiting for transfers between devices, same_x(): lax.all_to_all(value, 'expert', split_axis=0, concat_axis=0, axis_index_g...  10.8 us
    ppermute x3, waiting for transfers between devices, from_x(): return lax.ppermute(value, 'expert', pairs)  8.74 us
    unnamed x23, local copies, waits for them, and re-layouts  6.64 us
    ppermute x2, starting transfers between devices, swap_plane(): lax.ppermute(value, 'expert', [(e, (e + 16) % EXPERTS) for e in range(EXP...  6.62 us
    ppermute x4, waiting for transfers between devices, swap_y(): return lax.ppermute(value, 'replica', SWAP_Y)  6.35 us
    dot_general x1, matrix products, attend_local(): jnp.einsum('rgqd,rgpd->rgqp', queries, key_cache, preferred_element_type=...  5.75 us
  transfers between devices with their start and end apart: 15, of which 6 were waited for; matrix products, arithmetic and copies ran while one was open for 22% of the time, Pallas kernels for 0%

profile of v2, /device:TPU:0, one launch (start us, length us, event | category | flops | bytes accessed | tf_op | source)
XLA Modules:
  0.0 186.7 jit_solution(9644790323425403461)
XLA Ops:
  0.0 3.1 %collective-permute-start.3 = (bf16[256,1024]{1,0:T(8,128)(2,1)}, bf16[256,1024]{1,0:T(8,128)(2,1)S(1)}, u32[]{:S(2)}, u32[]{:S(2)}) collective-permute-start(bf16[256,1024]{1,0:T(8,128)(2,1)} %param.21), channel_id=1, source_target_pairs={{0,2},{1,3},{2,0},{3,1},{4,6},{5,7},{6,4},{7,5},{8,10},{9,11},{10,... | collective-permute-start | bytes 1572872 | tf_op jit(solution)/shard_map/ppermute | solution.py:81
  3.1 1.1 collective-permute-start.2
  4.2 0.9 collective-permute-start.4
  5.1 1.6 collective-permute-start.6
  6.7 0.7 iota_compare_fusion.2
  7.4 0.7 reshape.183
  8.2 1.0 copy.57
  9.4 5.7 %fusion.7 = (f32[16,4,16]{2,1,0:T(4,128)S(1)}, f32[16,4,16,512]{3,2,1,0:T(8,128)S(1)}) fusion(pred[16,512]{1,0:T(8,128)(4,1)S(1)} %iota_compare_fusion.2, bf16[16,4,16,128]{3,2,1,0:T(8,128)(2,1)S(1)} %bitcast.53, bf16[16,4,512,128]{3,2,1,0:T(8,128)(2,1)} %param.18), kind=kOutput, calls=%fused_computation.9 | convolution fusion | flops 135789568 | bytes 10760192 | tf_op jit(solution)/shard_map/rgqd,rgpd->rgqp/dot_general | solution.py:30
  15.2 1.3 copy-done.1
  16.5 0.8 fusion.8
  17.3 0.8 constant_dynamic-update-slice_fusion.3
  18.2 8.7 %collective-permute-done.2 = bf16[256,1024]{1,0:T(8,128)(2,1)} collective-permute-done((bf16[256,1024]{1,0:T(8,128)(2,1)}, bf16[256,1024]{1,0:T(8,128)(2,1)}, u32[]{:S(2)}, u32[]{:S(2)}) %collective-permute-start.2) | collective-permute-done | bytes 524320 | tf_op jit(solution)/shard_map/ppermute | solution.py:81
  26.9 1.9 %constant_dynamic-update-slice_fusion.2 = bf16[1024,1024]{1,0:T(8,128)(2,1)} fusion(bf16[1024,1024]{1,0:T(8,128)(2,1)} %constant_dynamic-update-slice_fusion.3, bf16[256,1024]{1,0:T(8,128)(2,1)} %collective-permute-done.2), kind=kLoop, calls=%fused_computation.85 | loop fusion | bytes 1048576
  28.8 0.9 constant_dynamic-update-slice_fusion.1
  29.7 1.9 %constant_dynamic-update-slice_fusion = bf16[1024,1024]{1,0:T(8,128)(2,1)} fusion(bf16[1024,1024]{1,0:T(8,128)(2,1)} %constant_dynamic-update-slice_fusion.1, bf16[256,1024]{1,0:T(8,128)(2,1)} %collective-permute-done.4), kind=kLoop, calls=%fused_computation.83 | loop fusion | bytes 1048576 | tf_op jit(solution)/shard_map/concatenate | solution.py:468
  31.6 5.7 %fusion.9 = bf16[16,4,16,128]{3,2,1,0:T(8,128)(2,1)} fusion(bf16[16,4,512,128]{3,2,1,0:T(8,128)(2,1)} %param.19, f32[16,4,16,512]{3,2,1,0:T(8,128)S(1)} %copy-done.2, f32[16,4,16]{2,1,0:T(4,128)S(1)} %get-tuple-element.16, f32[16,4,16]{2,1,0:T(4,128)S(1)} %multiply_maximum_fusion, pred[16,512]{1,0:T(8,128)(4,1)S(1)} %iota_compare_fusion.2, ...), kind=kOutput, calls=%fused_computation.12 | convolution fusion | flops 137232384 | bytes 10801152 | tf_op jit(solution)/shard_map/rgqp,rgpd->rgqd/dot_general | solution.py:50
  37.3 1.2 convert_element_type.54
  38.4 1.2 fusion.16
  39.6 1.1 reshape.184
  40.7 0.8 copy.59
  41.6 7.9 %all-to-all-start = ((bf16[8,16,1024]{2,1,0:T(8,128)(2,1)}), bf16[8,16,1024]{2,1,0:T(8,128)(2,1)}, u32[]{:S(2)}, u32[]{:S(2)}) async-start(bf16[8,16,1024]{2,1,0:T(8,128)(2,1)} %bitcast.48), calls=%async_computation | async-start | bytes 524288 | tf_op jit(solution)/shard_map/all_to_all | solution.py:72
  49.5 0.3 collective-permute-start.10
  49.8 0.3 collective-permute-start.11
  50.4 0.6 broadcast_select_fusion.15
  51.0 0.8 copy.43
  51.8 0.6 pad_maximum_fusion.3
  52.7 0.8 collective-permute-start.8
  53.4 0.7 fusion.45
  54.1 2.4 %collective-permute-done.8 = f32[16,8]{0,1:T(8,128)S(1)} collective-permute-done((f32[16,8]{0,1:T(8,128)}, f32[16,8]{0,1:T(8,128)S(1)}, u32[]{:S(2)}, u32[]{:S(2)}) %collective-permute-start.8) | collective-permute-done | bytes 544 | tf_op jit(solution)/shard_map/ppermute | solution.py:60
  56.6 3.3 %collective-permute-start.7 = (s32[2,16,8]{1,2,0:T(8,128)S(1)}, s32[2,16,8]{1,2,0:T(8,128)S(1)}, u32[]{:S(2)}, u32[]{:S(2)}) collective-permute-start(s32[2,16,8]{1,2,0:T(8,128)S(1)} %get-tuple-element.25), channel_id=1, source_target_pairs={{0,16},{1,17},{2,18},{3,19},{4,20},{5,21},{6,22},{7,23},{8,24},{9,... | collective-permute-start | bytes 3080 | tf_op jit(solution)/shard_map/ppermute | solution.py:68
  59.9 0.7 fusion.44
  60.6 0.8 copy.44
  61.4 0.3 collective-permute-done.7
  61.7 3.3 %collective-permute-start.9 = (f32[2,16,8]{1,2,0:T(8,128)S(1)}, f32[2,16,8]{1,2,0:T(8,128)S(1)}, u32[]{:S(2)}, u32[]{:S(2)}) collective-permute-start(f32[2,16,8]{1,2,0:T(8,128)S(1)} %get-tuple-element.23), channel_id=1, source_target_pairs={{0,16},{1,17},{2,18},{3,19},{4,20},{5,21},{6,22},{7,23},{8,24},{9,... | collective-permute-start | bytes 3080 | tf_op jit(solution)/shard_map/ppermute | solution.py:68
  65.2 1.7 collective-permute-done.9
  66.9 0.8 collective-permute-start.1
  67.8 0.8 fusion.17
  68.7 1.2 reduce_window_sum.11
  69.9 3.9 %collective-permute-done.1 = bf16[8,16,1024]{2,1,0:T(8,128)(2,1)} collective-permute-done((bf16[8,16,1024]{2,1,0:T(8,128)(2,1)}, bf16[8,16,1024]{2,1,0:T(8,128)(2,1)}, u32[]{:S(2)}, u32[]{:S(2)}) %collective-permute-start.1) | collective-permute-done | bytes 262176 | tf_op jit(solution)/shard_map/ppermute | solution.py:60
  73.8 0.6 collective-permute-start
  74.4 1.1 pad_maximum_fusion
  75.5 4.5 %fusion.4 = bf16[256,2048]{1,0:T(8,128)(2,1)} fusion(bf16[256,1024]{1,0:T(8,128)(2,1)S(1)} %bitcast.55, bf16[1024,1024]{1,0:T(8,128)(2,1)} %collective-permute-done.5, bf16[1024,1024]{1,0:T(8,128)(2,1)} %constant_dynamic-update-slice_fusion), kind=kOutput, calls=%fused_computation.4 | convolution fusion | flops 1082654720 | bytes 5767168 | tf_op jit(solution)/shard_map/dot_general | solution.py:508
  80.0 8.4 %all-to-all-start.1 = ((bf16[8,32,2048]{2,1,0:T(8,128)(2,1)}), bf16[8,32,2048]{2,1,0:T(8,128)(2,1)}, u32[]{:S(2)}, u32[]{:S(2)}) async-start(bf16[8,32,2048]{2,1,0:T(8,128)(2,1)} %bitcast.54), calls=%async_computation.1 | async-start | bytes 2097152 | tf_op jit(solution)/shard_map/all_to_all | solution.py:72
  89.5 10.8 %all-to-all-done.1 = bf16[8,32,2048]{2,1,0:T(8,128)(2,1)} async-done(((bf16[8,32,2048]{2,1,0:T(8,128)(2,1)}), bf16[8,32,2048]{2,1,0:T(8,128)(2,1)}, u32[]{:S(2)}, u32[]{:S(2)}) %all-to-all-start.1) | async-done | bytes 1048608 | tf_op jit(solution)/shard_map/all_to_all | solution.py:72
  100.3 1.4 convert_reduce_fusion
  101.8 0.9 convert_add_fusion.mid_ref
  102.7 83.3 %shard_map.136 = bf16[2,16,2048]{2,1,0:T(8,128)(2,1)S(1)} custom-call(f32[32,2048]{1,0:T(8,128)S(1)} %convert_add_fusion.mid_ref, f32[1,2048]{1,0:T(1,128)S(1)} %bitcast.50, bf16[2,256,32]{2,1,0:T(8,128)(2,1)S(1)} %bitcast.49, bf16[2,96,256]{2,1,0:T(8,128)(2,1)S(1)} %pad_maximum_fusion.2.weighting_ref, bf16[1024,1536]{1,0:T(8,128)(2,1)S(1)} %bitcast.51, ...), custom_call_target="tpu_custom_call" | custom-call | flops 10000000000 | bytes 20000000 | tf_op jit(solution)/shard_map/pallas_call | solution.py:395
  186.0 0.7 pad_maximum_fusion.1
  (60 shorter events, 2.5 us)
Async XLA Ops:
  0.0 28.8 %collective-permute-start.3 = (bf16[256,1024]{1,0:T(8,128)(2,1)}, bf16[256,1024]{1,0:T(8,128)(2,1)S(1)}, u32[]{:S(2)}, u32[]{:S(2)}) collective-permute-start(bf16[256,1024]{1,0:T(8,128)(2,1)} %param.21), channel_id=1, source_target_pairs={{0,2},{1,3},{2,0},{3,1},{4,6},{5,7},{6,4},{7,5},{8,10},{9,11},{10,... | collective-permute-start | bytes 1572872 | tf_op jit(solution)/shard_map/ppermute | solution.py:81
  3.1 23.8 %collective-permute-start.2 = (bf16[256,1024]{1,0:T(8,128)(2,1)}, bf16[256,1024]{1,0:T(8,128)(2,1)}, u32[]{:S(2)}, u32[]{:S(2)}) collective-permute-start(bf16[256,1024]{1,0:T(8,128)(2,1)} %param.21), channel_id=1, source_target_pairs={{0,3},{1,0},{2,1},{3,2},{4,7},{5,4},{6,5},{7,6},{8,11},{9,8},{10,9... | collective-permute-start | bytes 1572872 | tf_op jit(solution)/shard_map/ppermute | solution.py:81
  4.2 25.4 %collective-permute-start.4 = (bf16[256,1024]{1,0:T(8,128)(2,1)}, bf16[256,1024]{1,0:T(8,128)(2,1)}, u32[]{:S(2)}, u32[]{:S(2)}) collective-permute-start(bf16[256,1024]{1,0:T(8,128)(2,1)} %param.21), channel_id=1, source_target_pairs={{0,1},{1,2},{2,3},{3,0},{4,5},{5,6},{6,7},{7,4},{8,9},{9,10},{10,1... | collective-permute-start | bytes 1572872 | tf_op jit(solution)/shard_map/ppermute | solution.py:81
  5.1 47.5 %collective-permute-start.6 = (s32[16,8]{0,1:T(8,128)}, s32[16,8]{0,1:T(8,128)}, u32[]{:S(2)}, u32[]{:S(2)}) collective-permute-start(s32[16,8]{0,1:T(8,128)} %param.23), channel_id=1, source_target_pairs={{0,64},{32,96},{64,0},{96,32},{1,65},{33,97},{65,1},{97,33},{2,66}... | collective-permute-start | bytes 1544 | tf_op jit(solution)/shard_map/ppermute | solution.py:60
  15.2 1.4 copy-start.1
  15.2 2.1 %copy-start.3 = (bf16[256,1024]{1,0:T(8,128)(2,1)S(1)}, bf16[256,1024]{1,0:T(8,128)(2,1)}, u32[]{:S(2)}) copy-start(bf16[256,1024]{1,0:T(8,128)(2,1)} %param.21) | copy-start | bytes 1572868
  15.2 2.9 %copy-start.7 = (bf16[16,512]{1,0:T(8,128)(2,1)S(1)}, bf16[16,512]{1,0:T(8,128)(2,1)}, u32[]{:S(2)}) copy-start(bf16[16,512]{1,0:T(8,128)(2,1)} %param.17) | copy-start | bytes 49156
  18.1 13.4 %copy-start.2 = (f32[16,4,16,512]{3,2,1,0:T(8,128)S(1)}, f32[16,4,16,512]{3,2,1,0:T(8,128)}, u32[]{:S(2)}) copy-start(f32[16,4,16,512]{3,2,1,0:T(8,128)} %copy-done.1) | copy-start | bytes 6291460
  31.5 43.9 %collective-permute-start.5 = (bf16[1024,1024]{1,0:T(8,128)(2,1)}, bf16[1024,1024]{1,0:T(8,128)(2,1)}, u32[]{:S(2)}, u32[]{:S(2)}) collective-permute-start(bf16[1024,1024]{1,0:T(8,128)(2,1)} %constant_dynamic-update-slice_fusion), channel_id=1, source_target_pairs={{0,32},{32,0},{64,96},{96,64},{1,33},{33,1},{65,97},{97,65},{2,34}... | collective-permute-start | bytes 6291464 | tf_op jit(solution)/shard_map/ppermute | solution.py:64
  31.6 18.0 %copy-start = (bf16[1,1024,1536]{2,1,0:T(8,128)(2,1)S(1)}, bf16[1,1024,1536]{2,1,0:T(8,128)(2,1)}, u32[]{:S(2)}) copy-start(bf16[1,1024,1536]{2,1,0:T(8,128)(2,1)} %param.25) | copy-start | bytes 9437188
  37.3 13.1 %copy-start.8 = (f32[4096]{0:T(1024)S(1)}, f32[4096]{0:T(1024)}, u32[]{:S(2)}) copy-start(f32[4096]{0:T(1024)} %param.22) | copy-start | bytes 49156
  37.3 13.1 %copy-start.4 = (bf16[16,4096]{1,0:T(8,128)(2,1)S(1)}, bf16[16,4096]{1,0:T(8,128)(2,1)}, u32[]{:S(2)}) copy-start(bf16[16,4096]{1,0:T(8,128)(2,1)} %param.14) | copy-start | bytes 393220
  41.6 25.3 %all-to-all-start = ((bf16[8,16,1024]{2,1,0:T(8,128)(2,1)}), bf16[8,16,1024]{2,1,0:T(8,128)(2,1)}, u32[]{:S(2)}, u32[]{:S(2)}) async-start(bf16[8,16,1024]{2,1,0:T(8,128)(2,1)} %bitcast.48), calls=%async_computation | async-start | bytes 524288 | tf_op jit(solution)/shard_map/all_to_all | solution.py:72
  49.5 53.1 %collective-permute-start.10 = (bf16[1,1024,1536]{2,1,0:T(8,128)(2,1)S(1)}, bf16[1,1024,1536]{2,1,0:T(8,128)(2,1)}, u32[]{:S(2)}, u32[]{:S(2)}) collective-permute-start(bf16[1,1024,1536]{2,1,0:T(8,128)(2,1)S(1)} %copy-done), channel_id=1, source_target_pairs={{0,32},{32,0},{64,96},{96,64},{1,33},{33,1},{65,97},{97,65},{2,34}... | collective-permute-start | bytes 9437192 | tf_op jit(solution)/shard_map/ppermute | solution.py:64
  49.8 52.8 %collective-permute-start.11 = (bf16[1,1024,1536]{2,1,0:T(8,128)(2,1)}, bf16[1,1024,1536]{2,1,0:T(8,128)(2,1)}, u32[]{:S(2)}, u32[]{:S(2)}) collective-permute-start(bf16[1,1024,1536]{2,1,0:T(8,128)(2,1)} %param.26), channel_id=1, source_target_pairs={{0,32},{32,0},{64,96},{96,64},{1,33},{33,1},{65,97},{97,65},{2,34}... | collective-permute-start | bytes 9437192 | tf_op jit(solution)/shard_map/ppermute | solution.py:64
  50.1 52.5 %collective-permute-start.12 = (bf16[1,1536,1024]{2,1,0:T(8,128)(2,1)}, bf16[1,1536,1024]{2,1,0:T(8,128)(2,1)}, u32[]{:S(2)}, u32[]{:S(2)}) collective-permute-start(bf16[1,1536,1024]{2,1,0:T(8,128)(2,1)} %param.27), channel_id=1, source_target_pairs={{0,32},{32,0},{64,96},{96,64},{1,33},{33,1},{65,97},{97,65},{2,34}... | collective-permute-start | bytes 9437192 | tf_op jit(solution)/shard_map/ppermute | solution.py:64
  52.7 3.9 %collective-permute-start.8 = (f32[16,8]{0,1:T(8,128)}, f32[16,8]{0,1:T(8,128)S(1)}, u32[]{:S(2)}, u32[]{:S(2)}) collective-permute-start(f32[16,8]{0,1:T(8,128)} %param.24), channel_id=1, source_target_pairs={{0,64},{32,96},{64,0},{96,32},{1,65},{33,97},{65,1},{97,33},{2,66}... | collective-permute-start | bytes 1544 | tf_op jit(solution)/shard_map/ppermute | solution.py:60
  56.6 5.2 %collective-permute-start.7 = (s32[2,16,8]{1,2,0:T(8,128)S(1)}, s32[2,16,8]{1,2,0:T(8,128)S(1)}, u32[]{:S(2)}, u32[]{:S(2)}) collective-permute-start(s32[2,16,8]{1,2,0:T(8,128)S(1)} %get-tuple-element.25), channel_id=1, source_target_pairs={{0,16},{1,17},{2,18},{3,19},{4,20},{5,21},{6,22},{7,23},{8,24},{9,... | collective-permute-start | bytes 3080 | tf_op jit(solution)/shard_map/ppermute | solution.py:68
  61.7 5.2 %collective-permute-start.9 = (f32[2,16,8]{1,2,0:T(8,128)S(1)}, f32[2,16,8]{1,2,0:T(8,128)S(1)}, u32[]{:S(2)}, u32[]{:S(2)}) collective-permute-start(f32[2,16,8]{1,2,0:T(8,128)S(1)} %get-tuple-element.23), channel_id=1, source_target_pairs={{0,16},{1,17},{2,18},{3,19},{4,20},{5,21},{6,22},{7,23},{8,24},{9,... | collective-permute-start | bytes 3080 | tf_op jit(solution)/shard_map/ppermute | solution.py:68
  66.9 6.9 %collective-permute-start.1 = (bf16[8,16,1024]{2,1,0:T(8,128)(2,1)}, bf16[8,16,1024]{2,1,0:T(8,128)(2,1)}, u32[]{:S(2)}, u32[]{:S(2)}) collective-permute-start(bf16[8,16,1024]{2,1,0:T(8,128)(2,1)} %all-to-all-done), channel_id=1, source_target_pairs={{0,64},{32,96},{64,0},{96,32},{1,65},{33,97},{65,1},{97,33},{2,66}... | collective-permute-start | bytes 786440 | tf_op jit(solution)/shard_map/ppermute | solution.py:60
  73.8 27.9 %collective-permute-start = (bf16[16,2048]{1,0:T(8,128)(2,1)}, bf16[16,2048]{1,0:T(8,128)(2,1)}, u32[]{:S(2)}, u32[]{:S(2)}) collective-permute-start(bf16[16,2048]{1,0:T(8,128)(2,1)} %pad_maximum_fusion.3), channel_id=1, source_target_pairs={{0,64},{32,96},{64,0},{96,32},{1,65},{33,97},{65,1},{97,33},{2,66}... | collective-permute-start | bytes 196616 | tf_op jit(solution)/shard_map/ppermute | solution.py:60
  80.0 21.8 %copy-start.5 = (bf16[16,1024]{1,0:T(8,128)(2,1)S(1)}, bf16[16,1024]{1,0:T(8,128)(2,1)}, u32[]{:S(2)}) copy-start(bf16[16,1024]{1,0:T(8,128)(2,1)} %get-tuple-element.11) | copy-start | bytes 98308
  80.0 21.8 %copy-start.6 = (bf16[16,1024]{1,0:T(8,128)(2,1)S(1)}, bf16[16,1024]{1,0:T(8,128)(2,1)}, u32[]{:S(2)}) copy-start(bf16[16,1024]{1,0:T(8,128)(2,1)} %get-tuple-element.12) | copy-start | bytes 98308
  80.0 20.4 %all-to-all-start.1 = ((bf16[8,32,2048]{2,1,0:T(8,128)(2,1)}), bf16[8,32,2048]{2,1,0:T(8,128)(2,1)}, u32[]{:S(2)}, u32[]{:S(2)}) async-start(bf16[8,32,2048]{2,1,0:T(8,128)(2,1)} %bitcast.54), calls=%async_computation.1 | async-start | bytes 2097152 | tf_op jit(solution)/shard_map/all_to_all | solution.py:72

commit v3 on v0

v3 whole, which is shorter than its diff:
```python
import types

import jax
import jax.numpy as jnp
from jax import lax
from jax.experimental import pallas as pl
from jax.experimental.pallas import tpu as pltpu
from jax.sharding import PartitionSpec as P

HD = 128
TOP = 8
EXPERTS = 32
CAP = 8
ROWS = 16
RING = 8
TILE = 512
MESH = pl.DeviceIdType.MESH


def offset(s):
    dz = s % 8 // 2
    return dz, 2 * (s % 2) + (dz + s // 8) % 2


def shifted(expert, s, sign):
    dz, dx = offset(s)
    plane, z, x = expert // 16, expert // 4 % 4, expert % 4
    return plane * 16 + (z + 4 + sign * dz) % 4 * 4 + (x + 4 + sign * dx) % 4


def group_shifted(expert, t, sign):
    plane, z, x = expert // 16, expert // 4 % 4, expert % 4
    return (plane + t // 4) % 2 * 16 + (z + 4 + sign * (t % 4)) % 4 * 4 + x


def remote(src, dst, send, recv, device):
    return pltpu.make_async_remote_copy(
        src_ref=src,
        dst_ref=dst,
        send_sem=send,
        recv_sem=recv,
        device_id=device,
        device_id_type=MESH,
    )


def columns(n):
    return pl.ds(pl.multiple_of(n * TILE, TILE), TILE)


def scores_row(s, r, slot):
    groups = s.k_ring.shape[1]
    heads = s.q_rows.shape[1] // groups
    for g in range(groups):
        mine = pl.ds(g * heads, heads)
        s.scores[slot, mine, :] = lax.dot_general(
            s.q_rows[r, mine, :].astype(jnp.bfloat16),
            s.k_ring[slot, g],
            (((1,), (1,)), ((), ())),
            preferred_element_type=jnp.float32,
        )


def softmax_row(refs, s, r, slot):
    f32, bf16 = jnp.float32, jnp.bfloat16
    groups = s.k_ring.shape[1]
    heads = s.q_rows.shape[1] // groups
    scale = HD ** (-0.5)
    live = lax.broadcasted_iota(jnp.int32, s.scores.shape[1:], 1) < refs.cache_len[r]
    cached = jnp.where(live, s.scores[slot] * scale, -jnp.inf)
    own = [
        jnp.sum(
            s.q_rows[r, g * heads : (g + 1) * heads, :] * s.k_new[r, g : g + 1, :],
            axis=-1,
            keepdims=True,
        )
        for g in range(groups)
    ]
    own = jnp.concatenate(own, axis=0) * scale
    highest = jnp.maximum(jnp.max(cached, axis=-1, keepdims=True), own)
    cached_exp = jnp.exp(cached - highest)
    own_exp = jnp.exp(own - highest)
    inverse = 1.0 / (jnp.sum(cached_exp, axis=-1, keepdims=True) + own_exp)
    s.probs[slot] = (cached_exp * inverse).astype(bf16)
    own_prob = (own_exp * inverse).astype(bf16).astype(f32)
    for g in range(groups):
        mine = pl.ds(g * heads, heads)
        s.own_part[slot, mine, :] = (
            own_prob[g * heads : (g + 1) * heads] * s.v_new[r, g : g + 1, :]
        )


def values_row(s, r, slot):
    groups = s.k_ring.shape[1]
    heads = s.q_rows.shape[1] // groups
    for g in range(groups):
        mine = pl.ds(g * heads, heads)
        mixed = jnp.dot(
            s.probs[slot, mine, :], s.v_ring[slot, g], preferred_element_type=jnp.float32
        )
        s.o_rows[r, mine, :] = mixed + s.own_part[slot, mine, :]


def layer_kernel(names, scratch_names, *all_refs):
    refs = types.SimpleNamespace(**dict(zip(names, all_refs)))
    s = types.SimpleNamespace(**dict(zip(scratch_names, all_refs[len(names) :])))
    f32, bf16 = jnp.float32, jnp.bfloat16
    replica, expert = lax.axis_index("replica"), lax.axis_index("expert")
    plane, z, x = expert // 16, expert // 4 % 4, expert % 4
    sibling = replica // 2 * 2 + (replica + 1) % 2
    other_replica, other_plane = (replica + 2) % 4, (expert + 16) % 32
    other_sibling = other_replica // 2 * 2 + (other_replica + 1) % 2
    beside, across = (other_replica, expert), (replica, other_plane)
    diagonal, core = (other_replica, other_plane), (sibling, expert)
    line = expert // 4 * 4
    right, left = (replica, line + (x + 1) % 4), (replica, line + (x + 3) % 4)
    hidden, quarter = s.v_gate.shape[2], s.v_gate.shape[1]
    half = 2 * quarter
    n_rows = refs.cache_len.shape[0]
    deep = refs.attn_out_w.shape[0]

    def load_keys(r, slot):
        return pltpu.make_async_copy(refs.key_cache.at[r], s.k_ring.at[slot], s.k_sem.at[slot])

    def load_values(r, slot):
        return pltpu.make_async_copy(refs.value_cache.at[r], s.v_ring.at[slot], s.v_sem.at[slot])

    def proj_rows(block, start=0, count=deep):
        return pl.ds(pl.multiple_of(block * deep + start, 16), count)

    loads = [
        pltpu.make_async_copy(src, dst, s.load_sem.at[i])
        for i, (src, dst) in enumerate(
            [
                (refs.attn_out_w, s.v_proj.at[0, proj_rows(x)]),
                (refs.w_gate.at[0], s.v_gate.at[0]),
                (refs.w_up.at[0], s.v_up.at[0]),
                (refs.w_down.at[0], s.v_down.at[0]),
            ]
        )
    ]
    for r in range(RING):
        load_keys(r, r).start()
    loads[0].start()
    for r in range(RING):
        load_values(r, r).start()

    barrier = pltpu.get_barrier_semaphore()

    def greet(device):
        pl.semaphore_signal(barrier, inc=1, device_id=device, device_id_type=MESH)

    @pl.loop(1, 16)
    def _(i):
        greet((replica, shifted(expert, i, 1)))

    @pl.loop(1, 8)
    def _(t):
        greet((replica, group_shifted(expert, t, 1)))

    @pl.loop(0, 8)
    def _(t):
        greet((other_replica, group_shifted(expert, t, 1)))

    greet(core)

    for h in range(refs.query.shape[1] // HD):
        s.q_rows[:, h, :] = refs.query[:, h * HD : (h + 1) * HD].astype(f32)
    for g in range(refs.key_new.shape[1] // HD):
        s.k_new[:, g, :] = refs.key_new[:, g * HD : (g + 1) * HD].astype(f32)
        s.v_new[:, g, :] = refs.value_new[:, g * HD : (g + 1) * HD].astype(f32)

    square = (ROWS, ROWS)
    row_of = lax.broadcasted_iota(jnp.int32, square, 0)
    column_of = lax.broadcasted_iota(jnp.int32, square, 1)
    unit_matrix = jnp.where(row_of == column_of, 1.0, 0.0).astype(bf16)

    def turned(value):
        return lax.dot_general(
            unit_matrix, value, (((1,), (1,)), ((), ())), preferred_element_type=f32
        )

    routes = turned(refs.routes[...].astype(f32).astype(bf16)).astype(jnp.int32)
    rest = refs.gate_weights[...]
    gate_weights = jnp.zeros((ROWS, TOP), f32)
    for _ in range(3):
        piece = rest.astype(bf16)
        gate_weights = gate_weights + turned(piece)
        rest = rest - piece.astype(f32)
    lane = lax.broadcasted_iota(jnp.int32, (ROWS, 128), 1)
    named = jnp.zeros((ROWS, 128), f32)
    weight = jnp.zeros((ROWS, 128), f32)
    for k in range(TOP):
        hit = routes[:, k : k + 1] == lane % EXPERTS
        named = named + jnp.where(hit, 1.0, 0.0)
        weight = weight + jnp.where(hit, gate_weights[:, k : k + 1], 0.0)
    rank = jnp.dot(
        jnp.where(column_of < row_of, 1.0, 0.0).astype(bf16), named.astype(bf16), preferred_element_type=f32
    )
    high = weight.astype(bf16).astype(f32)
    middle = (weight - high).astype(bf16).astype(f32)
    kind = lane // EXPERTS
    s.info[0] = jnp.where(
        kind == 0,
        jnp.where(named > 0.0, rank, -1.0),
        jnp.where(kind == 1, high, jnp.where(kind == 2, middle, weight - high - middle)),
    )

    def quarter_of(q):
        return pl.ds(pl.multiple_of(q * quarter, quarter), quarter)

    s.hid_out[:, :quarter] = refs.hidden_in[:, quarter_of(other_replica)]
    s.hid_out[:, quarter:] = refs.hidden_in[:, quarter_of(other_sibling)]
    s.mid[:16, :quarter] = refs.hidden_in[:, quarter_of(replica)].astype(f32)
    s.mid[:16, quarter:] = refs.hidden_in[:, quarter_of(sibling)].astype(f32)
    s.gain[:, :quarter] = refs.norm_gain[:, quarter_of(replica)]
    s.gain[:, quarter:] = refs.norm_gain[:, quarter_of(sibling)]

    pl.semaphore_wait(barrier, 31)

    own_rows = s.v_proj.at[0, proj_rows(x)]
    to_right = remote(refs.attn_out_w, own_rows, s.x_send.at[0], s.x_recv.at[0], right)
    to_left = remote(refs.attn_out_w, own_rows, s.x_send.at[1], s.x_recv.at[1], left)
    to_core = [
        remote(
            refs.attn_out_w, s.v_proj.at[1, proj_rows(x)], s.core_send.at[0], s.core_recv.at[0], core
        )
    ]
    for i, (src, dst) in enumerate(
        [(refs.w_gate, s.v_gate), (refs.w_up, s.v_up), (refs.w_down, s.v_down)]
    ):
        to_core.append(
            remote(src.at[0], dst.at[1], s.core_send.at[i + 1], s.core_recv.at[i + 1], core)
        )
    early = [
        remote(s.info.at[0], s.info.at[2], s.early_send.at[0], s.early_recv.at[0], beside),
        remote(s.info.at[0], s.info.at[1], s.early_send.at[1], s.early_recv.at[1], across),
        remote(s.info.at[0], s.info.at[3], s.early_send.at[2], s.early_recv.at[2], diagonal),
        remote(s.hid_out, s.hid_in, s.early_send.at[3], s.early_recv.at[3], beside),
    ]
    for copy in [to_right, to_left] + early + to_core[:1]:
        copy.start()

    for b in range(n_rows // RING):
        last_turn = b == n_rows // RING - 1

        @pl.loop(0, RING, unroll=2)
        def _(i):
            load_keys(b * RING + i, i).wait()
            scores_row(s, b * RING + i, i)

        if not last_turn:
            for i in range(RING):
                load_keys((b + 1) * RING + i, i).start()

        @pl.loop(0, RING, unroll=2)
        def _(i):
            softmax_row(refs, s, b * RING + i, i)

        @pl.loop(0, RING, unroll=2)
        def _(i):
            load_values(b * RING + i, i).wait()
            values_row(s, b * RING + i, i)

        if not last_turn:
            for i in range(RING):
                load_values((b + 1) * RING + i, i).start()

    for copy in to_core[1:]:
        copy.start()
    for load in loads[1:]:
        load.start()

    to_right.wait_recv()
    to_left.wait_recv()
    mid_left, mid_right = proj_rows((x + 3) % 4, 0, deep // 2), proj_rows((x + 1) % 4, deep // 2, deep // 2)
    onward = [
        remote(s.v_proj.at[0, mid_left], s.v_proj.at[0, mid_left], s.x_send.at[2], s.x_recv.at[2], right),
        remote(s.v_proj.at[0, mid_right], s.v_proj.at[0, mid_right], s.x_send.at[3], s.x_recv.at[3], left),
    ]
    for step, i in ((1, 4), (3, 5), (2, 6)):
        rows = proj_rows((x + step) % 4)
        to_core.append(
            remote(
                s.v_proj.at[0, rows], s.v_proj.at[1, rows], s.core_send.at[i], s.core_recv.at[i], core
            )
        )
    for copy in onward + to_core[4:6]:
        copy.start()

    for h in range(s.o_rows.shape[1]):
        s.attn[h // 8, :, h % 8 * HD : (h % 8 + 1) * HD] = s.o_rows[:, h, :].astype(bf16)

    def heads_copy(t, h):
        there = group_shifted(expert, t, 1)
        return remote(
            s.attn.at[there // 4],
            s.heads.at[t, pl.ds(h * ROWS, ROWS)],
            s.heads_send.at[t, h],
            s.heads_recv.at[t, h],
            (other_replica if h else replica, there),
        )

    heads_copy(0, 1).start()

    @pl.loop(1, 8)
    def _(t):
        heads_copy(t, 0).start()
        heads_copy(t, 1).start()

    s.heads[0, :ROWS, :] = s.attn[expert // 4]
    for copy in onward:
        copy.wait_recv()
    to_core[6].start()

    for copy in early:
        copy.wait_recv()
    s.mid[16:, :] = s.hid_in[...].astype(f32)
    slot = lax.broadcasted_iota(jnp.int32, (128, 256), 1)
    step = slot // 16
    dz = step % 8 // 2
    dx = 2 * (step % 2) + (dz + step // 8) % 2
    taker = plane * 16 + (z + dz) % 4 * 4 + (x + dx) % 4
    entry = lax.broadcasted_iota(jnp.int32, (128, 256), 0)
    slot32 = lax.broadcasted_iota(jnp.int32, (32, 256), 1)
    row32 = lax.broadcasted_iota(jnp.int32, (32, 256), 0)
    for h in range(2):
        infos = s.info[2 * h : 2 * h + 2].reshape(32, 128).astype(bf16)
        picked = [
            jnp.dot(
                infos,
                jnp.where(entry == taker + EXPERTS * i, 1.0, 0.0).astype(bf16),
                preferred_element_type=f32,
            )
            for i in range(4)
        ]
        hit = (picked[0] == (slot32 % CAP).astype(f32)) & (slot32 // CAP % 2 == row32 // ROWS)
        s.placing[h] = jnp.where(hit, 1.0, 0.0).astype(bf16)
        for i in range(3):
            s.weighting[h, 32 * i : 32 * i + 32, :] = jnp.where(hit, picked[i + 1], 0.0).astype(bf16)

    def sums_copy(t):
        return remote(
            s.sums.at[t],
            s.sums_in.at[t],
            s.sums_send.at[t],
            s.sums_recv.at[t],
            (replica, group_shifted(expert, t, -1)),
        )

    loads[0].wait()
    to_core[0].wait_recv()
    for copy in to_core[4:]:
        copy.wait_recv()
    heads_copy(0, 1).wait_recv()
    for c in range(2):

        @pl.loop(max(1, 4 * c), 4 * c + 4)
        def _(t):
            heads_copy(t, 0).wait_recv()
            heads_copy(t, 1).wait_recv()

        for q in range(2):

            @pl.loop(0, quarter // TILE)
            def _(n):
                value = jnp.dot(
                    s.heads[4 * c : 4 * c + 4].reshape(128, quarter),
                    s.v_proj[q, :, columns(n)],
                    preferred_element_type=f32,
                )
                at = pl.multiple_of(q * quarter + n * TILE, TILE)
                s.sums[4 * c : 4 * c + 4, :, pl.ds(at, TILE)] = value.astype(bf16).reshape(4, 32, TILE)

        @pl.loop(max(1, 4 * c), 4 * c + 4)
        def _(t):
            sums_copy(t).start()

    @pl.loop(1, 8)
    def _(t):
        sums_copy(t).wait_recv()

    @pl.loop(0, half // TILE)
    def _(n):
        total = s.mid[:, columns(n)] + s.sums[0, :, columns(n)].astype(f32)
        for t in range(1, 8):
            total = total + s.sums_in[t, :, columns(n)].astype(f32)
        s.mid[:, columns(n)] = total

    mid = s.mid[...]
    s.square_out[...] = jnp.broadcast_to(jnp.sum(mid * mid, axis=-1, keepdims=True), (32, 128))
    s.scaled[...] = (mid * s.gain[...]).astype(bf16)
    pre = [
        remote(s.square_out, s.square_in.at[i], s.pre_send.at[i], s.pre_recv.at[i], device)
        for i, device in enumerate((beside, across, diagonal))
    ]
    pre.append(remote(s.scaled, s.scaled_in, s.pre_send.at[3], s.pre_recv.at[3], across))
    for copy in (pre[3], pre[0], pre[1], pre[2]):
        copy.start()
    for copy in pre:
        copy.wait_recv()
    for h in range(2):
        here, there = pl.ds(16 * h, 16), pl.ds(16 * (1 - h), 16)
        width = 2.0 * half
        total = s.square_out[here, :1] + s.square_in[0, there, :1]
        normed = s.mid[here, :] * s.gain[...] * lax.rsqrt(total / width + 1e-06)
        s.rows_all[h, :16, :] = normed.astype(bf16)
        total = s.square_in[1, here, :1] + s.square_in[2, there, :1]
        normed = s.scaled_in[here, :].astype(f32) * lax.rsqrt(total / width + 1e-06)
        s.rows_all[h, 16:, :] = normed.astype(bf16)

    def dispatch(h, i):
        rows = pl.ds(pl.multiple_of(i * 16, 16), 16)
        return remote(
            s.outgoing.at[h, rows],
            s.block.at[h, rows],
            s.disp_send.at[h, i],
            s.disp_recv.at[h, i],
            (replica, shifted(expert, i, 1)),
        )

    for h in (1, 0):

        @pl.loop(0, half // TILE)
        def _(n):
            cols = pl.ds(pl.multiple_of(n * TILE, TILE), TILE)
            s.outgoing[h, :, cols] = lax.dot_general(
                s.placing[h],
                s.rows_all[h, :, cols],
                (((0,), (0,)), ((), ())),
                preferred_element_type=f32,
            ).astype(bf16)

        @pl.loop(1, 16)
        def _(i):
            dispatch(h, i).start()

        s.block[h, :16, :] = s.outgoing[h, :16, :]

    tiles = hidden // TILE

    def gate_up(h, start, count, n):
        rows, cols = pl.ds(start, count), columns(n)
        for which, mats in enumerate((s.v_gate, s.v_up)):
            yield which, jnp.dot(
                s.block[h, rows, :quarter], mats[0, :, cols], preferred_element_type=f32
            ) + jnp.dot(s.block[h, rows, quarter:], mats[1, :, cols], preferred_element_type=f32)

    def part_copy(c, n):
        return remote(
            s.part_out.at[c, n],
            s.part_in.at[c, n],
            s.part_send.at[c, n],
            s.part_recv.at[c, n],
            beside,
        )

    loads[1].wait()
    loads[2].wait()
    to_core[1].wait_recv()
    to_core[2].wait_recv()
    for c in range(2):

        @pl.loop(max(1, 8 * c), 8 * c + 8)
        def _(i):
            dispatch(1, i).wait_recv()

        @pl.loop(0, tiles)
        def _(n):
            for which, value in gate_up(1, 128 * c, 128, n):
                s.part_out[c, n, which] = value.astype(bf16)
            part_copy(c, n).start()

    @pl.loop(1, 16)
    def _(i):
        dispatch(0, i).wait_recv()

    @pl.loop(0, tiles)
    def _(n):
        for which, value in gate_up(0, 0, 256, n):
            s.part_own[n, which] = value

    def give_back(h, i):
        rows = pl.ds(pl.multiple_of(i * 16, 16), 16)
        return remote(
            s.result.at[h, rows],
            s.returned.at[h, rows],
            s.ret_send.at[h, i],
            s.ret_recv.at[h, i],
            (replica, shifted(expert, i, -1)),
        )

    def down(h, c):
        for q in range(2):

            @pl.loop(0, quarter // TILE)
            def _(n):
                value = jnp.zeros((128, TILE), f32)
                for k in range(tiles):
                    value = value + jnp.dot(
                        s.units[h, c, k],
                        s.v_down[q, k * TILE : (k + 1) * TILE, columns(n)],
                        preferred_element_type=f32,
                    )
                at = pl.multiple_of(q * quarter + n * TILE, TILE)
                s.result[h, pl.ds(128 * c, 128), pl.ds(at, TILE)] = value.astype(bf16)

        @pl.loop(max(1, 8 * c), 8 * c + 8)
        def _(i):
            give_back(h, i).start()

        if c == 0:
            s.returned[h, :16, :] = s.result[h, :16, :]

    def unit_copy(c, n):
        return remote(
            s.units.at[0, c, n],
            s.units.at[1, c, n],
            s.unit_send.at[c, n],
            s.unit_recv.at[c, n],
            beside,
        )

    def combine(h, c):
        @pl.loop(max(1, 8 * c), 8 * c + 8)
        def _(i):
            give_back(h, i).wait_recv()

        @pl.loop(0, half // TILE)
        def _(n):
            three = jnp.dot(
                s.weighting[h, :, 128 * c : 128 * c + 128],
                s.returned[h, 128 * c : 128 * c + 128, columns(n)],
                preferred_element_type=f32,
            )
            value = three[:32] + three[32:64] + three[64:]
            s.mixed[h, :, columns(n)] = value if c == 0 else s.mixed[h, :, columns(n)] + value

    for c in range(2):

        @pl.loop(0, tiles)
        def _(n):
            part_copy(c, n).wait_recv()
            rows = pl.ds(128 * c, 128)
            gate = s.part_own[n, 0, rows, :] + s.part_in[c, n, 0].astype(f32)
            up_val = s.part_own[n, 1, rows, :] + s.part_in[c, n, 1].astype(f32)
            s.units[0, c, n] = (gate / (1.0 + jnp.exp(-gate)) * up_val).astype(bf16)
            unit_copy(c, n).start()

        if c == 0:
            loads[3].wait()
            to_core[3].wait_recv()
        down(0, c)
    last = [
        remote(s.last_out.at[i], s.last_in.at[i], s.last_send.at[i], s.last_recv.at[i], device)
        for i, device in enumerate((across, beside, diagonal))
    ]
    for c in range(2):

        @pl.loop(0, tiles)
        def _(n):
            unit_copy(c, n).wait_recv()

        down(1, c)
        if c == 0:
            combine(0, 0)
            combine(0, 1)
            s.last_out[0] = s.mixed[0, 16:, :].astype(bf16)
            last[0].start()
            combine(1, 0)
    combine(1, 1)
    s.last_out[1] = (s.mid[16:, :] + s.mixed[1, :16, :]).astype(bf16)
    s.last_out[2] = s.mixed[1, 16:, :].astype(bf16)
    last[1].start()
    last[2].start()
    for copy in last:
        copy.wait_recv()
    here = s.mid[:16, :] + s.mixed[0, :16, :]
    refs.near_sum[:, quarter_of(replica)] = here[:, :quarter]
    refs.near_sum[:, quarter_of(sibling)] = here[:, quarter:]
    there = s.last_in[1].astype(f32)
    refs.near_sum[:, quarter_of(other_replica)] = there[:, :quarter]
    refs.near_sum[:, quarter_of(other_sibling)] = there[:, quarter:]
    refs.far_sum[:, quarter_of(replica)] = s.last_in[0, :, :quarter]
    refs.far_sum[:, quarter_of(sibling)] = s.last_in[0, :, quarter:]
    refs.far_sum[:, quarter_of(other_replica)] = s.last_in[2, :, :quarter]
    refs.far_sum[:, quarter_of(other_sibling)] = s.last_in[2, :, quarter:]

    heads_copy(0, 1).wait_send()

    @pl.loop(1, 8)
    def _(t):
        heads_copy(t, 0).wait_send()
        heads_copy(t, 1).wait_send()
        sums_copy(t).wait_send()

    for copy in [to_right, to_left] + early + to_core + onward + pre + last:
        copy.wait_send()
    for h in range(2):

        @pl.loop(1, 16)
        def _(i):
            dispatch(h, i).wait_send()
            give_back(h, i).wait_send()

    for c in range(2):

        @pl.loop(0, tiles)
        def _(n):
            part_copy(c, n).wait_send()
            unit_copy(c, n).wait_send()


ARGS = (
    "hidden_in",
    "query",
    "key_new",
    "value_new",
    "key_cache",
    "value_cache",
    "cache_len",
    "attn_out_w",
    "norm_gain",
    "routes",
    "gate_weights",
    "w_gate",
    "w_up",
    "w_down",
)


def body(*args):
    f32, bf16 = jnp.float32, jnp.bfloat16
    given = dict(zip(ARGS, args))
    given["norm_gain"] = given["norm_gain"][None, :]
    given["routes"], given["gate_weights"] = given["routes"].T, given["gate_weights"].T
    n_rows, width = given["hidden_in"].shape
    groups, context, head_size = given["key_cache"].shape[1:]
    heads = given["query"].shape[1] // head_size
    _, quarter, hidden = given["w_gate"].shape
    deep = given["attn_out_w"].shape[0]
    half, tiles = 2 * quarter, hidden // TILE
    vmem, anywhere = pl.BlockSpec(memory_space=pltpu.VMEM), pl.BlockSpec(memory_space=pl.ANY)
    places = {name: vmem for name in ARGS}
    for name in ("key_cache", "value_cache", "attn_out_w", "w_gate", "w_up", "w_down"):
        places[name] = anywhere
    places["cache_len"] = pl.BlockSpec(memory_space=pltpu.SMEM)
    scratch = dict(
        k_ring=((RING, groups, context, head_size), bf16),
        v_ring=((RING, groups, context, head_size), bf16),
        q_rows=((n_rows, heads, head_size), f32),
        o_rows=((n_rows, heads, head_size), f32),
        scores=((RING, heads, context), f32),
        probs=((RING, heads, context), bf16),
        own_part=((RING, heads, head_size), f32),
        k_new=((n_rows, groups, head_size), f32),
        v_new=((n_rows, groups, head_size), f32),
        info=((4, ROWS, 128), f32),
        hid_out=((ROWS, half), bf16),
        hid_in=((ROWS, half), bf16),
        mid=((32, half), f32),
        gain=((1, half), f32),
        v_proj=((2, 4 * deep, quarter), bf16),
        v_gate=((2, quarter, hidden), bf16),
        v_up=((2, quarter, hidden), bf16),
        v_down=((2, hidden, quarter), bf16),
        attn=((8, ROWS, quarter), bf16),
        heads=((8, 32, quarter), bf16),
        sums=((8, 32, half), bf16),
        sums_in=((8, 32, half), bf16),
        placing=((2, 32, 256), bf16),
        weighting=((2, 96, 256), bf16),
        square_out=((32, 128), f32),
        square_in=((3, 32, 128), f32),
        scaled=((32, half), bf16),
        scaled_in=((32, half), bf16),
        rows_all=((2, 32, half), bf16),
        outgoing=((2, 256, half), bf16),
        block=((2, 256, half), bf16),
        part_out=((2, tiles, 2, 128, TILE), bf16),
        part_in=((2, tiles, 2, 128, TILE), bf16),
        part_own=((tiles, 2, 256, TILE), f32),
        units=((2, 2, tiles, 128, TILE), bf16),
        result=((2, 256, half), bf16),
        returned=((2, 256, half), bf16),
        mixed=((2, 32, half), f32),
        last_out=((3, 16, half), bf16),
        last_in=((3, 16, half), bf16),
    )
    semaphores = dict(
        k_sem=(RING,),
        v_sem=(RING,),
        load_sem=(4,),
        x_send=(4,),
        x_recv=(4,),
        core_send=(7,),
        core_recv=(7,),
        early_send=(4,),
        early_recv=(4,),
        heads_send=(8, 2),
        heads_recv=(8, 2),
        sums_send=(8,),
        sums_recv=(8,),
        pre_send=(4,),
        pre_recv=(4,),
        disp_send=(2, 16),
        disp_recv=(2, 16),
        part_send=(2, tiles),
        part_recv=(2, tiles),
        unit_send=(2, tiles),
        unit_recv=(2, tiles),
        ret_send=(2, 16),
        ret_recv=(2, 16),
        last_send=(3,),
        last_recv=(3,),
    )
    names = ARGS + ("near_sum", "far_sum")
    scratch_names = list(scratch) + list(semaphores)

    def kernel(*all_refs):
        layer_kernel(names, scratch_names, *all_refs)

    near_sum, far_sum = pl.pallas_call(
        kernel,
        out_shape=(
            jax.ShapeDtypeStruct((n_rows, width), f32),
            jax.ShapeDtypeStruct((n_rows, width), bf16),
        ),
        in_specs=[places[name] for name in ARGS],
        out_specs=(vmem, vmem),
        scratch_shapes=[pltpu.VMEM(*v) for v in scratch.values()]
        + [pltpu.SemaphoreType.DMA(v) for v in semaphores.values()],
        compiler_params=pltpu.CompilerParams(
            collective_id=0, has_side_effects=True, vmem_limit_bytes=60 * 1024 * 1024
        ),
        cost_estimate=pl.CostEstimate(
            flops=12 * 10**9, bytes_accessed=40 * 10**6, transcendentals=10**6
        ),
    )(*given.values())
    return (near_sum + far_sum.astype(f32)).astype(bf16)


def solution(mesh):
    placed = (
        P(("replica", "expert"), None),
        P(("replica", "expert"), None),
        P(("replica", "expert"), None),
        P(("replica", "expert"), None),
        P(("replica", "expert"), None, None, None),
        P(("replica", "expert"), None, None, None),
        P(("replica", "expert")),
        P("expert", "replica"),
        P(),
        P(("replica", "expert"), None),
        P(("replica", "expert"), None),
        P("expert", "replica", None),
        P("expert", "replica", None),
        P("expert", None, "replica"),
    )
    return jax.shard_map(
        body, mesh=mesh, in_specs=placed, out_specs=P(("replica", "expert"), None), check_vma=False
    )
```

time: 670 us -> 141 us (0.21)
  waiting for transfers between devices: 554 us -> 0 us
  Pallas kernels: 0 us -> 139 us
  blocking collectives: 43.9 us -> 0 us
  matrix products: 40 us -> 0 us
  between operations: 13.3 us -> 0.01 us
  starting transfers between devices: 10.1 us -> 0 us
    all_gather x4 -> x0, waiting for transfers between devices: 327 us -> none  [the longest x1 119 us: body(): lax.all_gather(w_up, 'replica', axis=1, tiled=True)]
    reduce_scatter x1 -> x0, waiting for transfers between devices: 194 us -> none  [body(): lax.psum_scatter(jnp.dot(head_rows, out_proj, preferred_element_type=jnp....]
    pallas_call x0 -> x1, Pallas kernels: none -> 139 us  [body(): pl.pallas_call(kernel, out_shape=(jax.ShapeDtypeStruct((n_rows, width), f...]
    all_to_all x2 -> x0, blocking collectives: 43.9 us -> none  [the longest x1 22.7 us: body(): lax.all_to_all(outgoing, 'expert', split_axis=1, concat_axis=1, tiled=True)]
    dot_general x8 -> x0, matrix products: 40 us -> none  [the longest x1 16.7 us: body(): jnp.einsum('lnch,lhd->lncd', units, down_full, preferred_element_type=jnp...]
    all_to_all x1 -> x0, waiting for transfers between devices: 30.6 us -> none  [send_back(): lax.all_to_all(values, 'expert', split_axis=1, concat_axis=1, tiled=True)]
    all_to_all x1 -> x0, starting transfers between devices: 9.96 us -> none  [send_back(): lax.all_to_all(values, 'expert', split_axis=1, concat_axis=1, tiled=True)]
  transfers between devices with their start and end apart: 6 -> 0, of which waited for: 6 -> 0; matrix products, arithmetic and copies ran while one was open for 3% -> 0% of each run, Pallas kernels for 0% -> 0%
where the time goes in v3:
time: 141 us
  Pallas kernels  139 us (99%)
  other arithmetic  1.66 us (1%)
    pallas_call x1, Pallas kernels, body(): pl.pallas_call(kernel, out_shape=(jax.ShapeDtypeStruct((n_rows, width), f...  139 us

profile of v3, /device:TPU:0, one launch (start us, length us, event | category | flops | bytes accessed | tf_op | source)
XLA Modules:
  0.0 141.1 jit_solution(13637087283428450618)
XLA Ops:
  0.0 139.4 %shard_map.136 = (f32[16,4096]{1,0:T(8,128)}, bf16[16,4096]{1,0:T(8,128)(2,1)}) custom-call(bf16[16,4096]{1,0:T(8,128)(2,1)} %all_refs_0_.1, bf16[16,8192]{1,0:T(8,128)(2,1)} %all_refs_1_.1, bf16[16,512]{1,0:T(8,128)(2,1)} %all_refs_2_.1, bf16[16,512]{1,0:T(8,128)(2,1)} %all_refs_3_.1, bf16[16,4,512,128]{3,2,1,0:T(8,128)(2,1)} %all_refs_4_.1, ...), custom_call_target="tpu_custom_call" | custom-call | flops 12000000000 | bytes 40000000 | tf_op jit(solution)/shard_map/pallas_call | solution.py:723
  139.4 1.7 %add_convert_fusion = bf16[16,4096]{1,0:T(8,128)(2,1)} fusion(f32[16,4096]{1,0:T(8,128)} %get-tuple-element.7, bf16[16,4096]{1,0:T(8,128)(2,1)} %get-tuple-element.8), kind=kLoop, calls=%fused_computation | loop fusion | flops 196608 | bytes 524288 | tf_op jit(solution)/shard_map/convert_element_type | solution.py:740

commit v4 on v3

--- a/solution.py
+++ b/solution.py
@@ -14,6 +14,8 @@
 ROWS = 16
 RING = 8
 TILE = 512
+CHUNKS = ((0, 8), (8, 8))
+SHARES = ((0, 8), (8, 4), (12, 4))
 MESH = pl.DeviceIdType.MESH
 
 
@@ -169,6 +171,44 @@
     for g in range(refs.key_new.shape[1] // HD):
         s.k_new[:, g, :] = refs.key_new[:, g * HD : (g + 1) * HD].astype(f32)
         s.v_new[:, g, :] = refs.value_new[:, g * HD : (g + 1) * HD].astype(f32)
+
+    def quarter_of(q):
+        return pl.ds(pl.multiple_of(q * quarter, quarter), quarter)
+
+    pl.semaphore_wait(barrier, 31)
+
+    half_deep = deep // 2
+
+    def x_copy(i, block, part, device):
+        rows = proj_rows(block, part * half_deep, half_deep)
+        src = refs.attn_out_w.at[pl.ds(part * half_deep, half_deep)] if i < 4 else s.v_proj.at[0, rows]
+        return remote(src, s.v_proj.at[0, rows], s.x_send.at[i], s.x_recv.at[i], device)
+
+    along = [
+        x_copy(0, x, 0, right),
+        x_copy(1, x, 1, left),
+        x_copy(2, x, 1, right),
+        x_copy(3, x, 0, left),
+    ]
+    to_core = [
+        remote(
+            refs.attn_out_w, s.v_proj.at[1, proj_rows(x)], s.core_send.at[0], s.core_recv.at[0], core
+        )
+    ]
+    for i, (src, dst) in enumerate(
+        [(refs.w_gate, s.v_gate), (refs.w_up, s.v_up), (refs.w_down, s.v_down)]
+    ):
+        to_core.append(
+            remote(src.at[0], dst.at[1], s.core_send.at[i + 1], s.core_recv.at[i + 1], core)
+        )
+    early = [
+        remote(s.info.at[0], s.info.at[2], s.early_send.at[0], s.early_recv.at[0], beside),
+        remote(s.info.at[0], s.info.at[1], s.early_send.at[1], s.early_recv.at[1], across),
+        remote(s.info.at[0], s.info.at[3], s.early_send.at[2], s.early_recv.at[2], diagonal),
+        remote(s.hid_out, s.hid_in, s.early_send.at[3], s.early_recv.at[3], beside),
+    ]
+    for copy in along + to_core[:1]:
+        copy.start()
 
     square = (ROWS, ROWS)
     row_of = lax.broadcasted_iota(jnp.int32, square, 0)
@@ -206,39 +246,13 @@
         jnp.where(kind == 1, high, jnp.where(kind == 2, middle, weight - high - middle)),
     )
 
-    def quarter_of(q):
-        return pl.ds(pl.multiple_of(q * quarter, quarter), quarter)
-
     s.hid_out[:, :quarter] = refs.hidden_in[:, quarter_of(other_replica)]
     s.hid_out[:, quarter:] = refs.hidden_in[:, quarter_of(other_sibling)]
     s.mid[:16, :quarter] = refs.hidden_in[:, quarter_of(replica)].astype(f32)
     s.mid[:16, quarter:] = refs.hidden_in[:, quarter_of(sibling)].astype(f32)
     s.gain[:, :quarter] = refs.norm_gain[:, quarter_of(replica)]
     s.gain[:, quarter:] = refs.norm_gain[:, quarter_of(sibling)]
-
-    pl.semaphore_wait(barrier, 31)
-
-    own_rows = s.v_proj.at[0, proj_rows(x)]
-    to_right = remote(refs.attn_out_w, own_rows, s.x_send.at[0], s.x_recv.at[0], right)
-    to_left = remote(refs.attn_out_w, own_rows, s.x_send.at[1], s.x_recv.at[1], left)
-    to_core = [
-        remote(
-            refs.attn_out_w, s.v_proj.at[1, proj_rows(x)], s.core_send.at[0], s.core_recv.at[0], core
-        )
-    ]
-    for i, (src, dst) in enumerate(
-        [(refs.w_gate, s.v_gate), (refs.w_up, s.v_up), (refs.w_down, s.v_down)]
-    ):
-        to_core.append(
-            remote(src.at[0], dst.at[1], s.core_send.at[i + 1], s.core_recv.at[i + 1], core)
-        )
-    early = [
-        remote(s.info.at[0], s.info.at[2], s.early_send.at[0], s.early_recv.at[0], beside),
-        remote(s.info.at[0], s.info.at[1], s.early_send.at[1], s.early_recv.at[1], across),
-        remote(s.info.at[0], s.info.at[3], s.early_send.at[2], s.early_recv.at[2], diagonal),
-        remote(s.hid_out, s.hid_in, s.early_send.at[3], s.early_recv.at[3], beside),
-    ]
-    for copy in [to_right, to_left] + early + to_core[:1]:
+    for copy in early:
         copy.start()
 
     for b in range(n_rows // RING):
@@ -265,53 +279,59 @@
         if not last_turn:
             for i in range(RING):
                 load_values((b + 1) * RING + i, i).start()
-
-    for copy in to_core[1:]:
+        if b == 0:
+            along[0].wait_recv()
+            along[1].wait_recv()
+            onward = [
+                x_copy(4, (x + 3) % 4, 0, right),
+                x_copy(5, (x + 1) % 4, 1, left),
+            ]
+            for copy in onward:
+                copy.start()
+
+
+    for h in range(s.o_rows.shape[1]):
+        s.attn[h // 8, :, h % 8 * HD : (h % 8 + 1) * HD] = s.o_rows[:, h, :].astype(bf16)
+
+    def heads_copy(h, t):
+        there = group_shifted(expert, t, 1)
+        return remote(
+            s.attn.at[there // 4],
+            s.heads.at[h, t],
+            s.heads_send.at[h, t],
+            s.heads_recv.at[h, t],
+            (other_replica if h else replica, there),
+        )
+
+    for h in (1, 0):
+
+        @pl.loop(1 - h, 8)
+        def _(t):
+            heads_copy(h, t).start()
+
+    s.heads[0, 0] = s.attn[expert // 4]
+
+    for copy in along[2:]:
+        copy.wait_recv()
+    for copy in onward:
+        copy.wait_recv()
+    for i, step in enumerate((1, 3, 2)):
+        rows = proj_rows((x + step) % 4)
+        to_core.append(
+            remote(
+                s.v_proj.at[0, rows],
+                s.v_proj.at[1, rows],
+                s.core_send.at[i + 4],
+                s.core_recv.at[i + 4],
+                core,
+            )
+        )
+        to_core[-1].start()
+
+    for copy in to_core[1:4]:
         copy.start()
     for load in loads[1:]:
         load.start()
-
-    to_right.wait_recv()
-    to_left.wait_recv()
-    mid_left, mid_right = proj_rows((x + 3) % 4, 0, deep // 2), proj_rows((x + 1) % 4, deep // 2, deep // 2)
-    onward = [
-        remote(s.v_proj.at[0, mid_left], s.v_proj.at[0, mid_left], s.x_send.at[2], s.x_recv.at[2], right),
-        remote(s.v_proj.at[0, mid_right], s.v_proj.at[0, mid_right], s.x_send.at[3], s.x_recv.at[3], left),
-    ]
-    for step, i in ((1, 4), (3, 5), (2, 6)):
-        rows = proj_rows((x + step) % 4)
-        to_core.append(
-            remote(
-                s.v_proj.at[0, rows], s.v_proj.at[1, rows], s.core_send.at[i], s.core_recv.at[i], core
-            )
-        )
-    for copy in onward + to_core[4:6]:
-        copy.start()
-
-    for h in range(s.o_rows.shape[1]):
-        s.attn[h // 8, :, h % 8 * HD : (h % 8 + 1) * HD] = s.o_rows[:, h, :].astype(bf16)
-
-    def heads_copy(t, h):
-        there = group_shifted(expert, t, 1)
-        return remote(
-            s.attn.at[there // 4],
-            s.heads.at[t, pl.ds(h * ROWS, ROWS)],
-            s.heads_send.at[t, h],
-            s.heads_recv.at[t, h],
-            (other_replica if h else replica, there),
-        )
-
-    heads_copy(0, 1).start()
-
-    @pl.loop(1, 8)
-    def _(t):
-        heads_copy(t, 0).start()
-        heads_copy(t, 1).start()
-
-    s.heads[0, :ROWS, :] = s.attn[expert // 4]
-    for copy in onward:
-        copy.wait_recv()
-    to_core[6].start()
 
     for copy in early:
         copy.wait_recv()
@@ -339,12 +359,12 @@
         for i in range(3):
             s.weighting[h, 32 * i : 32 * i + 32, :] = jnp.where(hit, picked[i + 1], 0.0).astype(bf16)
 
-    def sums_copy(t):
+    def sums_copy(h, t):
         return remote(
-            s.sums.at[t],
-            s.sums_in.at[t],
-            s.sums_send.at[t],
-            s.sums_recv.at[t],
+            s.sums.at[h, t],
+            s.sums_in.at[h, t],
+            s.sums_send.at[h, t],
+            s.sums_recv.at[h, t],
             (replica, group_shifted(expert, t, -1)),
         )
 
@@ -352,62 +372,59 @@
     to_core[0].wait_recv()
     for copy in to_core[4:]:
         copy.wait_recv()
-    heads_copy(0, 1).wait_recv()
-    for c in range(2):
-
-        @pl.loop(max(1, 4 * c), 4 * c + 4)
+    for h in (1, 0):
+
+        @pl.loop(1 - h, 8)
         def _(t):
-            heads_copy(t, 0).wait_recv()
-            heads_copy(t, 1).wait_recv()
+            heads_copy(h, t).wait_recv()
 
         for q in range(2):
 
             @pl.loop(0, quarter // TILE)
             def _(n):
                 value = jnp.dot(
-                    s.heads[4 * c : 4 * c + 4].reshape(128, quarter),
+                    s.heads[h].reshape(8 * ROWS, quarter),
                     s.v_proj[q, :, columns(n)],
                     preferred_element_type=f32,
                 )
                 at = pl.multiple_of(q * quarter + n * TILE, TILE)
-                s.sums[4 * c : 4 * c + 4, :, pl.ds(at, TILE)] = value.astype(bf16).reshape(4, 32, TILE)
-
-        @pl.loop(max(1, 4 * c), 4 * c + 4)
+                s.sums[h, :, :, pl.ds(at, TILE)] = value.astype(bf16).reshape(8, ROWS, TILE)
+
+        @pl.loop(1, 8)
         def _(t):
-            sums_copy(t).start()
-
-    @pl.loop(1, 8)
-    def _(t):
-        sums_copy(t).wait_recv()
-
-    @pl.loop(0, half // TILE)
-    def _(n):
-        total = s.mid[:, columns(n)] + s.sums[0, :, columns(n)].astype(f32)
-        for t in range(1, 8):
-            total = total + s.sums_in[t, :, columns(n)].astype(f32)
-        s.mid[:, columns(n)] = total
-
-    mid = s.mid[...]
-    s.square_out[...] = jnp.broadcast_to(jnp.sum(mid * mid, axis=-1, keepdims=True), (32, 128))
-    s.scaled[...] = (mid * s.gain[...]).astype(bf16)
-    pre = [
-        remote(s.square_out, s.square_in.at[i], s.pre_send.at[i], s.pre_recv.at[i], device)
-        for i, device in enumerate((beside, across, diagonal))
+            sums_copy(h, t).start()
+
+    over = [
+        remote(
+            s.rows_all.at[h, pl.ds(0, ROWS)],
+            s.rows_all.at[h, pl.ds(ROWS, ROWS)],
+            s.over_send.at[h],
+            s.over_recv.at[h],
+            across,
+        )
+        for h in range(2)
     ]
-    pre.append(remote(s.scaled, s.scaled_in, s.pre_send.at[3], s.pre_recv.at[3], across))
-    for copy in (pre[3], pre[0], pre[1], pre[2]):
-        copy.start()
-    for copy in pre:
-        copy.wait_recv()
-    for h in range(2):
-        here, there = pl.ds(16 * h, 16), pl.ds(16 * (1 - h), 16)
-        width = 2.0 * half
-        total = s.square_out[here, :1] + s.square_in[0, there, :1]
-        normed = s.mid[here, :] * s.gain[...] * lax.rsqrt(total / width + 1e-06)
-        s.rows_all[h, :16, :] = normed.astype(bf16)
-        total = s.square_in[1, here, :1] + s.square_in[2, there, :1]
-        normed = s.scaled_in[here, :].astype(f32) * lax.rsqrt(total / width + 1e-06)
-        s.rows_all[h, 16:, :] = normed.astype(bf16)
+
+    def finish_rows(h):
+        @pl.loop(1, 8)
+        def _(t):
+            sums_copy(h, t).wait_recv()
+
+        rows = pl.ds(ROWS * h, ROWS)
+
+        @pl.loop(0, half // TILE)
+        def _(n):
+            total = s.mid[rows, columns(n)] + s.sums[h, 0, :, columns(n)].astype(f32)
+            for t in range(1, 8):
+                total = total + s.sums_in[h, t, :, columns(n)].astype(f32)
+            s.mid[rows, columns(n)] = total
+            s.rows_all[h, :ROWS, columns(n)] = (total * s.gain[:, columns(n)]).astype(bf16)
+
+        over[h].start()
+        mid = s.mid[rows, :]
+        s.square_out[rows, :] = jnp.broadcast_to(
+            jnp.sum(mid * mid, axis=-1, keepdims=True), (ROWS, 128)
+        )
 
     def dispatch(h, i):
         rows = pl.ds(pl.multiple_of(i * 16, 16), 16)
@@ -419,66 +436,133 @@
             (replica, shifted(expert, i, 1)),
         )
 
-    for h in (1, 0):
-
-        @pl.loop(0, half // TILE)
-        def _(n):
-            cols = pl.ds(pl.multiple_of(n * TILE, TILE), TILE)
-            s.outgoing[h, :, cols] = lax.dot_general(
-                s.placing[h],
-                s.rows_all[h, :, cols],
-                (((0,), (0,)), ((), ())),
-                preferred_element_type=f32,
-            ).astype(bf16)
+    def send_rows(h):
+        over[h].wait_recv()
+        for first, number in CHUNKS:
+            slots = pl.ds(16 * first, 16 * number)
+
+            @pl.loop(0, half // TILE)
+            def _(n):
+                s.outgoing[h, slots, columns(n)] = lax.dot_general(
+                    s.placing[h, :, slots],
+                    s.rows_all[h, :, columns(n)],
+                    (((0,), (0,)), ((), ())),
+                    preferred_element_type=f32,
+                ).astype(bf16)
+
+            @pl.loop(max(1, first), first + number)
+            def _(i):
+                dispatch(h, i).start()
+
+            if first == 0:
+                s.block[h, :16, :] = s.outgoing[h, :16, :]
+
+    finish_rows(1)
+    send_rows(1)
+    finish_rows(0)
+    squares = [
+        remote(
+            s.square_out, s.square_in.at[i], s.square_send.at[i], s.square_recv.at[i], device
+        )
+        for i, device in enumerate((beside, across, diagonal))
+    ]
+    for copy in squares:
+        copy.start()
+    send_rows(0)
+
+    def scale_copy(i):
+        slots = pl.ds(pl.multiple_of(i * 16, 16), 16)
+        return remote(
+            s.scale_out.at[slots],
+            s.scale_in.at[slots],
+            s.scale_send.at[i],
+            s.scale_recv.at[i],
+            (replica, shifted(expert, i, 1)),
+        )
+
+    def send_scales():
+        for copy in squares:
+            copy.wait_recv()
+        total = jnp.concatenate(
+            [
+                s.square_out[:ROWS, :] + s.square_in[0, ROWS:, :],
+                s.square_in[1, :ROWS, :] + s.square_in[2, ROWS:, :],
+            ],
+            axis=0,
+        )
+        rest = lax.rsqrt(total / (2.0 * half) + 1e-06)
+        value = jnp.zeros((256, 128), f32)
+        for _ in range(3):
+            piece = rest.astype(bf16)
+            value = value + lax.dot_general(
+                s.placing[0], piece, (((0,), (0,)), ((), ())), preferred_element_type=f32
+            )
+            rest = rest - piece.astype(f32)
+        s.scale_out[...] = value
 
         @pl.loop(1, 16)
         def _(i):
-            dispatch(h, i).start()
-
-        s.block[h, :16, :] = s.outgoing[h, :16, :]
+            scale_copy(i).start()
+
+        s.scale_in[:16, :] = value[:16]
 
     tiles = hidden // TILE
 
-    def gate_up(h, start, count, n):
-        rows, cols = pl.ds(start, count), columns(n)
+    def slots_of(c, chunks=CHUNKS):
+        first, number = chunks[c]
+        return pl.ds(16 * first, 16 * number)
+
+    def gate_up(h, c, n):
         for which, mats in enumerate((s.v_gate, s.v_up)):
             yield which, jnp.dot(
-                s.block[h, rows, :quarter], mats[0, :, cols], preferred_element_type=f32
-            ) + jnp.dot(s.block[h, rows, quarter:], mats[1, :, cols], preferred_element_type=f32)
+                s.block[h, slots_of(c), :quarter],
+                mats[0, :, columns(n)],
+                preferred_element_type=f32,
+            ) + jnp.dot(
+                s.block[h, slots_of(c), quarter:],
+                mats[1, :, columns(n)],
+                preferred_element_type=f32,
+            )
 
     def part_copy(c, n):
         return remote(
-            s.part_out.at[c, n],
-            s.part_in.at[c, n],
+            s.part_out.at[n, :, slots_of(c)],
+            s.part_in.at[n, :, slots_of(c)],
             s.part_send.at[c, n],
             s.part_recv.at[c, n],
             beside,
         )
+
+    def wait_rows(h, c):
+        first, number = CHUNKS[c]
+
+        @pl.loop(max(1, first), first + number)
+        def _(i):
+            dispatch(h, i).wait_recv()
 
     loads[1].wait()
     loads[2].wait()
     to_core[1].wait_recv()
     to_core[2].wait_recv()
-    for c in range(2):
-
-        @pl.loop(max(1, 8 * c), 8 * c + 8)
-        def _(i):
-            dispatch(1, i).wait_recv()
+    for c in range(len(CHUNKS)):
+        wait_rows(1, c)
 
         @pl.loop(0, tiles)
         def _(n):
-            for which, value in gate_up(1, 128 * c, 128, n):
-                s.part_out[c, n, which] = value.astype(bf16)
+            for which, value in gate_up(1, c, n):
+                s.part_out[n, which, slots_of(c), :] = value.astype(bf16)
             part_copy(c, n).start()
 
-    @pl.loop(1, 16)
-    def _(i):
-        dispatch(0, i).wait_recv()
-
-    @pl.loop(0, tiles)
-    def _(n):
-        for which, value in gate_up(0, 0, 256, n):
-            s.part_own[n, which] = value
+        if c == 0:
+            send_scales()
+
+    def own_part(c):
+        wait_rows(0, c)
+
+        @pl.loop(0, tiles)
+        def _(n):
+            for which, value in gate_up(0, c, n):
+                s.part_own[n, which, slots_of(c), :] = value
 
     def give_back(h, i):
         rows = pl.ds(pl.multiple_of(i * 16, 16), 16)
@@ -490,85 +574,102 @@
             (replica, shifted(expert, i, -1)),
         )
 
-    def down(h, c):
+    def down(h, c, chunks):
+        first, number = chunks[c]
         for q in range(2):
 
             @pl.loop(0, quarter // TILE)
             def _(n):
-                value = jnp.zeros((128, TILE), f32)
+                value = jnp.zeros((16 * number, TILE), f32)
                 for k in range(tiles):
                     value = value + jnp.dot(
-                        s.units[h, c, k],
+                        s.units[h, k, slots_of(c, chunks), :],
                         s.v_down[q, k * TILE : (k + 1) * TILE, columns(n)],
                         preferred_element_type=f32,
                     )
                 at = pl.multiple_of(q * quarter + n * TILE, TILE)
-                s.result[h, pl.ds(128 * c, 128), pl.ds(at, TILE)] = value.astype(bf16)
-
-        @pl.loop(max(1, 8 * c), 8 * c + 8)
+                s.result[h, slots_of(c, chunks), pl.ds(at, TILE)] = value.astype(bf16)
+
+        @pl.loop(max(1, first), first + number)
         def _(i):
             give_back(h, i).start()
 
-        if c == 0:
+        if first == 0:
             s.returned[h, :16, :] = s.result[h, :16, :]
 
     def unit_copy(c, n):
         return remote(
-            s.units.at[0, c, n],
-            s.units.at[1, c, n],
+            s.units.at[0, n, slots_of(c, SHARES)],
+            s.units.at[1, n, slots_of(c, SHARES)],
             s.unit_send.at[c, n],
             s.unit_recv.at[c, n],
             beside,
         )
 
-    def combine(h, c):
-        @pl.loop(max(1, 8 * c), 8 * c + 8)
+    def combine(h, begin, end):
+        @pl.loop(max(1, begin), end)
         def _(i):
             give_back(h, i).wait_recv()
+
+        slots = pl.ds(16 * begin, 16 * (end - begin))
 
         @pl.loop(0, half // TILE)
         def _(n):
             three = jnp.dot(
-                s.weighting[h, :, 128 * c : 128 * c + 128],
-                s.returned[h, 128 * c : 128 * c + 128, columns(n)],
+                s.weighting[h, :, slots],
+                s.returned[h, slots, columns(n)],
                 preferred_element_type=f32,
             )
             value = three[:32] + three[32:64] + three[64:]
-            s.mixed[h, :, columns(n)] = value if c == 0 else s.mixed[h, :, columns(n)] + value
-
-    for c in range(2):
+            s.mixed[h, :, columns(n)] = value if begin == 0 else s.mixed[h, :, columns(n)] + value
+
+    @pl.loop(1, 16)
+    def _(i):
+        scale_copy(i).wait_recv()
+
+    own_part(0)
+    for c in range(len(CHUNKS)):
 
         @pl.loop(0, tiles)
         def _(n):
             part_copy(c, n).wait_recv()
-            rows = pl.ds(128 * c, 128)
-            gate = s.part_own[n, 0, rows, :] + s.part_in[c, n, 0].astype(f32)
-            up_val = s.part_own[n, 1, rows, :] + s.part_in[c, n, 1].astype(f32)
-            s.units[0, c, n] = (gate / (1.0 + jnp.exp(-gate)) * up_val).astype(bf16)
+            scale = s.scale_in[slots_of(c), :1]
+            gate = s.part_own[n, 0, slots_of(c), :] + s.part_in[n, 0, slots_of(c), :].astype(f32)
+            up_val = s.part_own[n, 1, slots_of(c), :] + s.part_in[n, 1, slots_of(c), :].astype(f32)
+            gate, up_val = gate * scale, up_val * scale
+            s.units[0, n, slots_of(c), :] = (gate / (1.0 + jnp.exp(-gate)) * up_val).astype(bf16)
             unit_copy(c, n).start()
+
+        if c == 1:
+
+            @pl.loop(0, tiles)
+            def _(n):
+                unit_copy(2, n).start()
 
         if c == 0:
             loads[3].wait()
             to_core[3].wait_recv()
-        down(0, c)
+        if c + 1 < len(CHUNKS):
+            own_part(c + 1)
+        down(0, c, CHUNKS)
     last = [
         remote(s.last_out.at[i], s.last_in.at[i], s.last_send.at[i], s.last_recv.at[i], device)
         for i, device in enumerate((across, beside, diagonal))
     ]
-    for c in range(2):
+    for c in range(len(SHARES)):
 
         @pl.loop(0, tiles)
         def _(n):
             unit_copy(c, n).wait_recv()
 
-        down(1, c)
+        down(1, c, SHARES)
         if c == 0:
-            combine(0, 0)
-            combine(0, 1)
+            combine(0, 0, 16)
             s.last_out[0] = s.mixed[0, 16:, :].astype(bf16)
             last[0].start()
-            combine(1, 0)
-    combine(1, 1)
+            combine(1, 0, 8)
+    combine(1, 8, 12)
+    combine(1, 12, 16)
     s.last_out[1] = (s.mid[16:, :] + s.mixed[1, :16, :]).astype(bf16)
     s.last_out[2] = s.mixed[1, 16:, :].astype(bf16)
     last[1].start()
@@ -586,28 +687,37 @@
     refs.far_sum[:, quarter_of(other_replica)] = s.last_in[2, :, :quarter]
     refs.far_sum[:, quarter_of(other_sibling)] = s.last_in[2, :, quarter:]
 
-    heads_copy(0, 1).wait_send()
-
-    @pl.loop(1, 8)
-    def _(t):
-        heads_copy(t, 0).wait_send()
-        heads_copy(t, 1).wait_send()
-        sums_copy(t).wait_send()
-
-    for copy in [to_right, to_left] + early + to_core + onward + pre + last:
+    for copy in along + early + to_core + onward + over + squares + last:
         copy.wait_send()
     for h in range(2):
+
+        @pl.loop(1 - h, 8)
+        def _(t):
+            heads_copy(h, t).wait_send()
+
+        @pl.loop(1, 8)
+        def _(t):
+            sums_copy(h, t).wait_send()
 
         @pl.loop(1, 16)
         def _(i):
             dispatch(h, i).wait_send()
             give_back(h, i).wait_send()
 
-    for c in range(2):
+    @pl.loop(1, 16)
+    def _(i):
+        scale_copy(i).wait_send()
+
+    for c in range(len(CHUNKS)):
 
         @pl.loop(0, tiles)
         def _(n):
             part_copy(c, n).wait_send()
+
+    for c in range(len(SHARES)):
+
+        @pl.loop(0, tiles)
+        def _(n):
             unit_copy(c, n).wait_send()
 
 
@@ -665,22 +775,22 @@
         v_up=((2, quarter, hidden), bf16),
         v_down=((2, hidden, quarter), bf16),
         attn=((8, ROWS, quarter), bf16),
-        heads=((8, 32, quarter), bf16),
-        sums=((8, 32, half), bf16),
-        sums_in=((8, 32, half), bf16),
+        heads=((2, 8, ROWS, quarter), bf16),
+        sums=((2, 8, ROWS, half), bf16),
+        sums_in=((2, 8, ROWS, half), bf16),
         placing=((2, 32, 256), bf16),
         weighting=((2, 96, 256), bf16),
         square_out=((32, 128), f32),
         square_in=((3, 32, 128), f32),
-        scaled=((32, half), bf16),
-        scaled_in=((32, half), bf16),
+        scale_out=((256, 128), f32),
+        scale_in=((256, 128), f32),
         rows_all=((2, 32, half), bf16),
         outgoing=((2, 256, half), bf16),
         block=((2, 256, half), bf16),
-        part_out=((2, tiles, 2, 128, TILE), bf16),
-        part_in=((2, tiles, 2, 128, TILE), bf16),
+        part_out=((tiles, 2, 256, TILE), bf16),
+        part_in=((tiles, 2, 256, TILE), bf16),
         part_own=((tiles, 2, 256, TILE), f32),
-        units=((2, 2, tiles, 128, TILE), bf16),
+        units=((2, tiles, 256, TILE), bf16),
         result=((2, 256, half), bf16),
         returned=((2, 256, half), bf16),
         mixed=((2, 32, half), f32),
@@ -691,24 +801,28 @@
         k_sem=(RING,),
         v_sem=(RING,),
         load_sem=(4,),
-        x_send=(4,),
-        x_recv=(4,),
+        x_send=(6,),
+        x_recv=(6,),
         core_send=(7,),
         core_recv=(7,),
         early_send=(4,),
         early_recv=(4,),
-        heads_send=(8, 2),
-        heads_recv=(8, 2),
-        sums_send=(8,),
-        sums_recv=(8,),
-        pre_send=(4,),
-        pre_recv=(4,),
+        heads_send=(2, 8),
+        heads_recv=(2, 8),
+        sums_send=(2, 8),
+        sums_recv=(2, 8),
+        over_send=(2,),
+        over_recv=(2,),
+        square_send=(3,),
+        square_recv=(3,),
+        scale_send=(16,),
+        scale_recv=(16,),
         disp_send=(2, 16),
         disp_recv=(2, 16),
-        part_send=(2, tiles),
-        part_recv=(2, tiles),
-        unit_send=(2, tiles),
-        unit_recv=(2, tiles),
+        part_send=(len(CHUNKS), tiles),
+        part_recv=(len(CHUNKS), tiles),
+        unit_send=(len(SHARES), tiles),
+        unit_recv=(len(SHARES), tiles),
         ret_send=(2, 16),
         ret_recv=(2, 16),
         last_send=(3,),

time: 141 us -> 135 us (0.957)
  Pallas kernels: 139 us -> 133 us
    pallas_call x1, Pallas kernels: 139 us -> 133 us  [body(): pl.pallas_call(kernel, out_shape=(jax.ShapeDtypeStruct((n_rows, width), f...]
where the time goes in v4:
time: 135 us
  Pallas kernels  133 us (99%)
  other arithmetic  1.66 us (1%)
    pallas_call x1, Pallas kernels, body(): pl.pallas_call(kernel, out_shape=(jax.ShapeDtypeStruct((n_rows, width), f...  133 us

profile of v4, /device:TPU:0, one launch (start us, length us, event | category | flops | bytes accessed | tf_op | source)
XLA Modules:
  0.0 135.2 jit_solution(5110440323523248054)
XLA Ops:
  0.0 133.5 %shard_map.136 = (f32[16,4096]{1,0:T(8,128)}, bf16[16,4096]{1,0:T(8,128)(2,1)}) custom-call(bf16[16,4096]{1,0:T(8,128)(2,1)} %all_refs_0_.1, bf16[16,8192]{1,0:T(8,128)(2,1)} %all_refs_1_.1, bf16[16,512]{1,0:T(8,128)(2,1)} %all_refs_2_.1, bf16[16,512]{1,0:T(8,128)(2,1)} %all_refs_3_.1, bf16[16,4,512,128]{3,2,1,0:T(8,128)(2,1)} %all_refs_4_.1, ...), custom_call_target="tpu_custom_call" | custom-call | flops 12000000000 | bytes 40000000 | tf_op jit(solution)/shard_map/pallas_call | solution.py:837
  133.5 1.7 %add_convert_fusion = bf16[16,4096]{1,0:T(8,128)(2,1)} fusion(f32[16,4096]{1,0:T(8,128)} %get-tuple-element.7, bf16[16,4096]{1,0:T(8,128)(2,1)} %get-tuple-element.8), kind=kLoop, calls=%fused_computation | loop fusion | flops 196608 | bytes 524288 | tf_op jit(solution)/shard_map/convert_element_type | solution.py:854

commit v5 on v4

--- a/solution.py
+++ b/solution.py
@@ -121,6 +121,32 @@
     n_rows = refs.cache_len.shape[0]
     deep = refs.attn_out_w.shape[0]
 
+    barrier = pltpu.get_barrier_semaphore()
+
+    def greet(device):
+        pl.semaphore_signal(barrier, inc=1, device_id=device, device_id_type=MESH)
+
+    @pl.loop(1, 16)
+    def _(i):
+        greet((replica, shifted(expert, i, 1)))
+
+    @pl.loop(1, 8)
+    def _(t):
+        greet((replica, group_shifted(expert, t, 1)))
+
+    @pl.loop(0, 8)
+    def _(t):
+        greet((other_replica, group_shifted(expert, t, 1)))
+
+    greet(core)
+
+    small = [
+        pltpu.make_async_copy(getattr(refs, name), getattr(s, "in_" + name), s.small_sem.at[i])
+        for i, name in enumerate(SMALL)
+    ]
+    for copy in small:
+        copy.start()
+
     def load_keys(r, slot):
         return pltpu.make_async_copy(refs.key_cache.at[r], s.k_ring.at[slot], s.k_sem.at[slot])
 
@@ -147,31 +173,6 @@
     for r in range(RING):
         load_values(r, r).start()
 
-    barrier = pltpu.get_barrier_semaphore()
-
-    def greet(device):
-        pl.semaphore_signal(barrier, inc=1, device_id=device, device_id_type=MESH)
-
-    @pl.loop(1, 16)
-    def _(i):
-        greet((replica, shifted(expert, i, 1)))
-
-    @pl.loop(1, 8)
-    def _(t):
-        greet((replica, group_shifted(expert, t, 1)))
-
-    @pl.loop(0, 8)
-    def _(t):
-        greet((other_replica, group_shifted(expert, t, 1)))
-
-    greet(core)
-
-    for h in range(refs.query.shape[1] // HD):
-        s.q_rows[:, h, :] = refs.query[:, h * HD : (h + 1) * HD].astype(f32)
-    for g in range(refs.key_new.shape[1] // HD):
-        s.k_new[:, g, :] = refs.key_new[:, g * HD : (g + 1) * HD].astype(f32)
-        s.v_new[:, g, :] = refs.value_new[:, g * HD : (g + 1) * HD].astype(f32)
-
     def quarter_of(q):
         return pl.ds(pl.multiple_of(q * quarter, quarter), quarter)
 
@@ -210,6 +211,14 @@
     for copy in along + to_core[:1]:
         copy.start()
 
+    for copy in small:
+        copy.wait()
+    for h in range(s.in_query.shape[1] // HD):
+        s.q_rows[:, h, :] = s.in_query[:, h * HD : (h + 1) * HD].astype(f32)
+    for g in range(s.in_key_new.shape[1] // HD):
+        s.k_new[:, g, :] = s.in_key_new[:, g * HD : (g + 1) * HD].astype(f32)
+        s.v_new[:, g, :] = s.in_value_new[:, g * HD : (g + 1) * HD].astype(f32)
+
     square = (ROWS, ROWS)
     row_of = lax.broadcasted_iota(jnp.int32, square, 0)
     column_of = lax.broadcasted_iota(jnp.int32, square, 1)
@@ -220,8 +229,8 @@
             unit_matrix, value, (((1,), (1,)), ((), ())), preferred_element_type=f32
         )
 
-    routes = turned(refs.routes[...].astype(f32).astype(bf16)).astype(jnp.int32)
-    rest = refs.gate_weights[...]
+    routes = turned(s.in_routes[...].astype(f32).astype(bf16)).astype(jnp.int32)
+    rest = s.in_gate_weights[...]
     gate_weights = jnp.zeros((ROWS, TOP), f32)
     for _ in range(3):
         piece = rest.astype(bf16)
@@ -246,13 +255,13 @@
         jnp.where(kind == 1, high, jnp.where(kind == 2, middle, weight - high - middle)),
     )
 
-    s.hid_out[:, :quarter] = refs.hidden_in[:, quarter_of(other_replica)]
-    s.hid_out[:, quarter:] = refs.hidden_in[:, quarter_of(other_sibling)]
-    s.mid[:16, :quarter] = refs.hidden_in[:, quarter_of(replica)].astype(f32)
-    s.mid[:16, quarter:] = refs.hidden_in[:, quarter_of(sibling)].astype(f32)
-    s.gain[:, :quarter] = refs.norm_gain[:, quarter_of(replica)]
-    s.gain[:, quarter:] = refs.norm_gain[:, quarter_of(sibling)]
-    for copy in early:
+    s.hid_out[:, :quarter] = s.in_hidden_in[:, quarter_of(other_replica)]
+    s.hid_out[:, quarter:] = s.in_hidden_in[:, quarter_of(other_sibling)]
+    s.mid[:16, :quarter] = s.in_hidden_in[:, quarter_of(replica)].astype(f32)
+    s.mid[:16, quarter:] = s.in_hidden_in[:, quarter_of(sibling)].astype(f32)
+    s.gain[:, :quarter] = s.in_norm_gain[:, quarter_of(replica)]
+    s.gain[:, quarter:] = s.in_norm_gain[:, quarter_of(sibling)]
+    for copy in early + to_core[1:2]:
         copy.start()
 
     for b in range(n_rows // RING):
@@ -286,7 +295,7 @@
                 x_copy(4, (x + 3) % 4, 0, right),
                 x_copy(5, (x + 1) % 4, 1, left),
             ]
-            for copy in onward:
+            for copy in onward + to_core[2:3]:
                 copy.start()
 
 
@@ -328,8 +337,6 @@
         )
         to_core[-1].start()
 
-    for copy in to_core[1:4]:
-        copy.start()
     for load in loads[1:]:
         load.start()
 
@@ -372,6 +379,7 @@
     to_core[0].wait_recv()
     for copy in to_core[4:]:
         copy.wait_recv()
+    to_core[3].start()
     for h in (1, 0):
 
         @pl.loop(1 - h, 8)
@@ -436,29 +444,30 @@
             (replica, shifted(expert, i, 1)),
         )
 
-    def send_rows(h):
-        over[h].wait_recv()
-        for first, number in CHUNKS:
-            slots = pl.ds(16 * first, 16 * number)
-
-            @pl.loop(0, half // TILE)
-            def _(n):
-                s.outgoing[h, slots, columns(n)] = lax.dot_general(
-                    s.placing[h, :, slots],
-                    s.rows_all[h, :, columns(n)],
-                    (((0,), (0,)), ((), ())),
-                    preferred_element_type=f32,
-                ).astype(bf16)
-
-            @pl.loop(max(1, first), first + number)
-            def _(i):
-                dispatch(h, i).start()
-
-            if first == 0:
-                s.block[h, :16, :] = s.outgoing[h, :16, :]
+    def send_rows(h, c):
+        if c == 0:
+            over[h].wait_recv()
+        first, number = CHUNKS[c]
+        slots = pl.ds(16 * first, 16 * number)
+
+        @pl.loop(0, half // TILE)
+        def _(n):
+            s.outgoing[h, slots, columns(n)] = lax.dot_general(
+                s.placing[h, :, slots],
+                s.rows_all[h, :, columns(n)],
+                (((0,), (0,)), ((), ())),
+                preferred_element_type=f32,
+            ).astype(bf16)
+
+        @pl.loop(max(1, first), first + number)
+        def _(i):
+            dispatch(h, i).start()
+
+        if first == 0:
+            s.block[h, :16, :] = s.outgoing[h, :16, :]
 
     finish_rows(1)
-    send_rows(1)
+    send_rows(1, 0)
     finish_rows(0)
     squares = [
         remote(
@@ -468,7 +477,8 @@
     ]
     for copy in squares:
         copy.start()
-    send_rows(0)
+    send_rows(1, 1)
+    send_rows(0, 0)
 
     def scale_copy(i):
         slots = pl.ds(pl.multiple_of(i * 16, 16), 16)
@@ -554,6 +564,7 @@
             part_copy(c, n).start()
 
         if c == 0:
+            send_rows(0, 1)
             send_scales()
 
     def own_part(c):
@@ -663,11 +674,37 @@
             unit_copy(c, n).wait_recv()
 
         down(1, c, SHARES)
-        if c == 0:
+        if c == 1:
             combine(0, 0, 16)
             s.last_out[0] = s.mixed[0, 16:, :].astype(bf16)
             last[0].start()
-            combine(1, 0, 8)
+    for copy in along + early + to_core + onward + over + squares:
+        copy.wait_send()
+
+    @pl.loop(1, 8)
+    def _(i):
+        heads_copy(0, i).wait_send()
+        heads_copy(1, i).wait_send()
+        sums_copy(0, i).wait_send()
+        sums_copy(1, i).wait_send()
+        give_back(1, i).wait_send()
+
+    heads_copy(1, 0).wait_send()
+
+    @pl.loop(1, 16)
+    def _(i):
+        dispatch(0, i).wait_send()
+        dispatch(1, i).wait_send()
+        scale_copy(i).wait_send()
+        give_back(0, i).wait_send()
+
+    @pl.loop(0, tiles)
+    def _(n):
+        part_copy(0, n).wait_send()
+        part_copy(1, n).wait_send()
+        unit_copy(0, n).wait_send()
+
+    combine(1, 0, 8)
     combine(1, 8, 12)
     combine(1, 12, 16)
     s.last_out[1] = (s.mid[16:, :] + s.mixed[1, :16, :]).astype(bf16)
@@ -687,38 +724,17 @@
     refs.far_sum[:, quarter_of(other_replica)] = s.last_in[2, :, :quarter]
     refs.far_sum[:, quarter_of(other_sibling)] = s.last_in[2, :, quarter:]
 
-    for copy in along + early + to_core + onward + over + squares + last:
+    for copy in last:
         copy.wait_send()
-    for h in range(2):
-
-        @pl.loop(1 - h, 8)
-        def _(t):
-            heads_copy(h, t).wait_send()
-
-        @pl.loop(1, 8)
-        def _(t):
-            sums_copy(h, t).wait_send()
-
-        @pl.loop(1, 16)
-        def _(i):
-            dispatch(h, i).wait_send()
-            give_back(h, i).wait_send()
-
-    @pl.loop(1, 16)
+
+    @pl.loop(8, 16)
     def _(i):
-        scale_copy(i).wait_send()
-
-    for c in range(len(CHUNKS)):
-
-        @pl.loop(0, tiles)
-        def _(n):
-            part_copy(c, n).wait_send()
-
-    for c in range(len(SHARES)):
-
-        @pl.loop(0, tiles)
-        def _(n):
-            unit_copy(c, n).wait_send()
+        give_back(1, i).wait_send()
+
+    @pl.loop(0, tiles)
+    def _(n):
+        unit_copy(1, n).wait_send()
+        unit_copy(2, n).wait_send()
 
 
 ARGS = (
@@ -739,6 +755,17 @@
 )
 
 
+SMALL = (
+    "query",
+    "key_new",
+    "value_new",
+    "routes",
+    "gate_weights",
+    "hidden_in",
+    "norm_gain",
+)
+
+
 def body(*args):
     f32, bf16 = jnp.float32, jnp.bfloat16
     given = dict(zip(ARGS, args))
@@ -751,11 +778,10 @@
     deep = given["attn_out_w"].shape[0]
     half, tiles = 2 * quarter, hidden // TILE
     vmem, anywhere = pl.BlockSpec(memory_space=pltpu.VMEM), pl.BlockSpec(memory_space=pl.ANY)
-    places = {name: vmem for name in ARGS}
-    for name in ("key_cache", "value_cache", "attn_out_w", "w_gate", "w_up", "w_down"):
-        places[name] = anywhere
+    places = {name: anywhere for name in ARGS}
     places["cache_len"] = pl.BlockSpec(memory_space=pltpu.SMEM)
-    scratch = dict(
+    scratch = {"in_" + name: (given[name].shape, given[name].dtype) for name in SMALL}
+    scratch |= dict(
         k_ring=((RING, groups, context, head_size), bf16),
         v_ring=((RING, groups, context, head_size), bf16),
         q_rows=((n_rows, heads, head_size), f32),
@@ -801,6 +827,7 @@
         k_sem=(RING,),
         v_sem=(RING,),
         load_sem=(4,),
+        small_sem=(len(SMALL),),
         x_send=(6,),
         x_recv=(6,),
         core_send=(7,),

time: 135 us -> 130 us (0.963)
  Pallas kernels: 133 us -> 128 us
    pallas_call x1, Pallas kernels: 133 us -> 128 us  [body(): pl.pallas_call(kernel, out_shape=(jax.ShapeDtypeStruct((n_rows, width), f...]
where the time goes in v5:
time: 130 us
  Pallas kernels  128 us (98%)
  other arithmetic  1.66 us (1%)
    pallas_call x1, Pallas kernels, body(): pl.pallas_call(kernel, out_shape=(jax.ShapeDtypeStruct((n_rows, width), f...  128 us

profile of v5, /device:TPU:0, one launch (start us, length us, event | category | flops | bytes accessed | tf_op | source)
XLA Modules:
  0.0 129.7 jit_solution(12210934374837858103)
XLA Ops:
  0.0 128.0 %shard_map.136 = (f32[16,4096]{1,0:T(8,128)}, bf16[16,4096]{1,0:T(8,128)(2,1)}) custom-call(bf16[16,4096]{1,0:T(8,128)(2,1)} %all_refs_0_.1, bf16[16,8192]{1,0:T(8,128)(2,1)} %all_refs_1_.1, bf16[16,512]{1,0:T(8,128)(2,1)} %all_refs_2_.1, bf16[16,512]{1,0:T(8,128)(2,1)} %all_refs_3_.1, bf16[16,4,512,128]{3,2,1,0:T(8,128)(2,1)} %all_refs_4_.1, ...), custom_call_target="tpu_custom_call" | custom-call | flops 12000000000 | bytes 40000000 | tf_op jit(solution)/shard_map/pallas_call | solution.py:864
  128.0 1.7 %add_convert_fusion = bf16[16,4096]{1,0:T(8,128)(2,1)} fusion(f32[16,4096]{1,0:T(8,128)} %get-tuple-element.7, bf16[16,4096]{1,0:T(8,128)(2,1)} %get-tuple-element.8), kind=kLoop, calls=%fused_computation | loop fusion | flops 196608 | bytes 524288 | tf_op jit(solution)/shard_map/convert_element_type | solution.py:881

commit v6 on v5

--- a/solution.py
+++ b/solution.py
@@ -208,7 +208,7 @@
         remote(s.info.at[0], s.info.at[3], s.early_send.at[2], s.early_recv.at[2], diagonal),
         remote(s.hid_out, s.hid_in, s.early_send.at[3], s.early_recv.at[3], beside),
     ]
-    for copy in along + to_core[:1]:
+    for copy in along[:2] + to_core[:1]:
         copy.start()
 
     for copy in small:
@@ -272,6 +272,9 @@
             load_keys(b * RING + i, i).wait()
             scores_row(s, b * RING + i, i)
 
+        if b == 0:
+            for copy in along[2:]:
+                copy.start()
         if not last_turn:
             for i in range(RING):
                 load_keys((b + 1) * RING + i, i).start()

time: 130 us -> 130 us (level)
  no operation moved by 1% of the time
where the time goes in v6:
time: 130 us
  Pallas kernels  128 us (98%)
  other arithmetic  1.66 us (1%)
    pallas_call x1, Pallas kernels, body(): pl.pallas_call(kernel, out_shape=(jax.ShapeDtypeStruct((n_rows, width), f...  128 us

profile of v6, /device:TPU:0, one launch (start us, length us, event | category | flops | bytes accessed | tf_op | source)
XLA Modules:
  0.0 129.7 jit_solution(18028653182344828527)
XLA Ops:
  0.0 128.0 %shard_map.136 = (f32[16,4096]{1,0:T(8,128)}, bf16[16,4096]{1,0:T(8,128)(2,1)}) custom-call(bf16[16,4096]{1,0:T(8,128)(2,1)} %all_refs_0_.1, bf16[16,8192]{1,0:T(8,128)(2,1)} %all_refs_1_.1, bf16[16,512]{1,0:T(8,128)(2,1)} %all_refs_2_.1, bf16[16,512]{1,0:T(8,128)(2,1)} %all_refs_3_.1, bf16[16,4,512,128]{3,2,1,0:T(8,128)(2,1)} %all_refs_4_.1, ...), custom_call_target="tpu_custom_call" | custom-call | flops 12000000000 | bytes 40000000 | tf_op jit(solution)/shard_map/pallas_call | solution.py:867
  128.0 1.7 %add_convert_fusion = bf16[16,4096]{1,0:T(8,128)(2,1)} fusion(f32[16,4096]{1,0:T(8,128)} %get-tuple-element.7, bf16[16,4096]{1,0:T(8,128)(2,1)} %get-tuple-element.8), kind=kLoop, calls=%fused_computation | loop fusion | flops 196608 | bytes 524288 | tf_op jit(solution)/shard_map/convert_element_type | solution.py:884

commit v7 on v6

--- a/solution.py
+++ b/solution.py
@@ -677,10 +677,9 @@
             unit_copy(c, n).wait_recv()
 
         down(1, c, SHARES)
-        if c == 1:
-            combine(0, 0, 16)
-            s.last_out[0] = s.mixed[0, 16:, :].astype(bf16)
-            last[0].start()
+    combine(0, 0, 16)
+    s.last_out[0] = s.mixed[0, 16:, :].astype(bf16)
+    last[0].start()
     for copy in along + early + to_core + onward + over + squares:
         copy.wait_send()
 

time: 130 us -> 129 us (level)
  no operation moved by 1% of the time
where the time goes in v7:
time: 129 us
  Pallas kernels  128 us (99%)
  other arithmetic  1.66 us (1%)
    pallas_call x1, Pallas kernels, body(): pl.pallas_call(kernel, out_shape=(jax.ShapeDtypeStruct((n_rows, width), f...  128 us

profile of v7, /device:TPU:0, one launch (start us, length us, event | category | flops | bytes accessed | tf_op | source)
XLA Modules:
  0.0 129.3 jit_solution(15500477579430734687)
XLA Ops:
  0.0 127.6 %shard_map.136 = (f32[16,4096]{1,0:T(8,128)}, bf16[16,4096]{1,0:T(8,128)(2,1)}) custom-call(bf16[16,4096]{1,0:T(8,128)(2,1)} %all_refs_0_.1, bf16[16,8192]{1,0:T(8,128)(2,1)} %all_refs_1_.1, bf16[16,512]{1,0:T(8,128)(2,1)} %all_refs_2_.1, bf16[16,512]{1,0:T(8,128)(2,1)} %all_refs_3_.1, bf16[16,4,512,128]{3,2,1,0:T(8,128)(2,1)} %all_refs_4_.1, ...), custom_call_target="tpu_custom_call" | custom-call | flops 12000000000 | bytes 40000000 | tf_op jit(solution)/shard_map/pallas_call | solution.py:866
  127.6 1.7 %add_convert_fusion = bf16[16,4096]{1,0:T(8,128)(2,1)} fusion(f32[16,4096]{1,0:T(8,128)} %get-tuple-element.7, bf16[16,4096]{1,0:T(8,128)(2,1)} %get-tuple-element.8), kind=kLoop, calls=%fused_computation | loop fusion | flops 196608 | bytes 524288 | tf_op jit(solution)/shard_map/convert_element_type | solution.py:883
